TPU v7x, 512 devices: a whole 4x4x16 slice. The times are simulated.
512 devices in a mesh: gx: 32 (over z, core), gy: 16 (over x, y).
Axes of the slice: x: 4, y: 4, z: 16, core: 2. Of those that a mesh axis runs over, the one named last changes fastest.
Arguments:
- source: float32 [128, 512, 128], P('gx', 'gy'), may hold values from -7 to 7
- beta: float32 [128, 512, 128], P('gx', 'gy'), may hold values from 0.5 to 4
- shift_field: float32 [128, 512, 128], P('gx', 'gy'), may hold values from 0.001 to 0.1
Outputs:
- correction: float32 [128, 512, 128], P('gx', 'gy')
All inputs are finite; a program needn't handle non-finite values.
Results may differ from a plain program's by a relative error of at most 0.0001.
Values sent between devices are 32-bit elements; how exact they have to be, the bound alone decides.
A program may use at most 64 MiB of HBM per device.

v0:
```python
import jax
import jax.numpy as jnp
from jax import lax
from jax.sharding import PartitionSpec as P

ITERS = 6


FIRST = 1.0 / 1.2
CARRY = 2.0 / 7.0
SECOND = 0.75 / 0.7
VERTICAL = 1.0 / 16.0
PLANE_SCALES = (1.0, 0.25, 0.0625)


def extended(block, sides, width):
    for axis, dim in sides:
        count = lax.axis_size(axis)
        forward = [(i, i + 1) for i in range(count - 1)]
        backward = [(target, source) for source, target in forward]
        low = lax.ppermute(
            lax.slice_in_dim(block, block.shape[dim] - width, None, axis=dim), axis, forward
        )
        high = lax.ppermute(lax.slice_in_dim(block, 0, width, axis=dim), axis, backward)
        block = jnp.concatenate([low, block, high], axis=dim)
    return block


def weights_of(beta_ext, plane_scale):
    centre = beta_ext[1:-1, 1:-1, :]
    z_padded = jnp.pad(centre, ((0, 0), (0, 0), (1, 1)))
    plane = 0.5 * plane_scale
    upright = 0.5 * VERTICAL
    return (
        plane * (centre + beta_ext[2:, 1:-1, :]),
        plane * (centre + beta_ext[:-2, 1:-1, :]),
        plane * (centre + beta_ext[1:-1, 2:, :]),
        plane * (centre + beta_ext[1:-1, :-2, :]),
        upright * (centre + z_padded[:, :, 2:]),
        upright * (centre + z_padded[:, :, :-2]),
    )


def operate(field_ext, shift_term, weights):
    centre = field_ext[1:-1, 1:-1, :]
    z_padded = jnp.pad(centre, ((0, 0), (0, 0), (1, 1)))
    result = shift_term * centre
    result = result + weights[0] * (centre - field_ext[2:, 1:-1, :])
    result = result + weights[1] * (centre - field_ext[:-2, 1:-1, :])
    result = result + weights[2] * (centre - field_ext[1:-1, 2:, :])
    result = result + weights[3] * (centre - field_ext[1:-1, :-2, :])
    result = result + weights[4] * (centre - z_padded[:, :, 2:])
    result = result + weights[5] * (centre - z_padded[:, :, :-2])
    return result


def diagonal_of(shift_term, weights):
    return shift_term + weights[0] + weights[1] + weights[2] + weights[3] + weights[4] + weights[5]


def coarsen(field):
    height, width, depth = field.shape
    return field.reshape(height // 2, 2, width // 2, 2, depth).mean(axis=(1, 3))


def prolong(field):
    return jnp.repeat(jnp.repeat(field, 2, axis=0), 2, axis=1)


def rims(field):
    return extended(field, (("gx", 0), ("gy", 1)), 1)


def prepare(beta_level, shift_term, plane_scale):
    beta_ext = extended(beta_level, (("gx", 0), ("gy", 1)), 1)
    weights = weights_of(beta_ext, plane_scale)
    return (shift_term, weights, diagonal_of(shift_term, weights), None)


def presmooth(rhs, level):
    shift_term, weights, diagonal, wide_parts = level
    first_step = FIRST * rhs / diagonal
    second_resid = rhs - operate(rims(first_step), shift_term, weights)
    return first_step + (CARRY * first_step + SECOND * second_resid / diagonal)


def postsmooth(iterate, rhs, level):
    shift_term, weights, diagonal, wide_parts = level
    first_resid = rhs - operate(rims(iterate), shift_term, weights)
    first_step = FIRST * first_resid / diagonal
    moved = iterate + first_step
    second_resid = rhs - operate(rims(moved), shift_term, weights)
    return moved + (CARRY * first_step + SECOND * second_resid / diagonal)


def squares(residual):
    return lax.psum(jnp.sum(residual * residual), ("gx", "gy"))


def on_device(source, beta, shift_field):
    fine_level = prepare(beta, shift_field, PLANE_SCALES[0])
    middle_beta = coarsen(beta)
    middle_shift = coarsen(shift_field)
    middle_level = prepare(middle_beta, middle_shift, PLANE_SCALES[1])
    coarse_beta = coarsen(middle_beta)
    coarse_shift = coarsen(middle_shift)
    coarse_ext = extended(coarse_beta, (("gx", 0), ("gy", 1)), 1)
    coarse_weights = weights_of(coarse_ext, PLANE_SCALES[2])
    fine_iter = presmooth(source, fine_level)
    middle_rhs = coarsen(source - operate(rims(fine_iter), fine_level[0], fine_level[1]))
    middle_iter = presmooth(middle_rhs, middle_level)
    coarse_rhs = coarsen(middle_rhs - operate(rims(middle_iter), middle_level[0], middle_level[1]))
    coarse_sol = jnp.zeros_like(coarse_rhs)
    residual = coarse_rhs
    direction = coarse_rhs
    norm_now = squares(residual)
    for turn_index in range(ITERS):
        image = operate(rims(direction), coarse_shift, coarse_weights)
        alpha = norm_now / lax.psum(jnp.sum(direction * image), ("gx", "gy"))
        coarse_sol = coarse_sol + alpha * direction
        residual = residual - alpha * image
        norm_next = squares(residual)
        direction = residual + norm_next / norm_now * direction
        norm_now = norm_next
    middle_iter = postsmooth(middle_iter + prolong(coarse_sol), middle_rhs, middle_level)
    return postsmooth(fine_iter + prolong(middle_iter), source, fine_level)


def solution(mesh):
    placed = (P("gx", "gy", None), P("gx", "gy", None), P("gx", "gy", None))
    return jax.shard_map(
        on_device, mesh=mesh, in_specs=placed, out_specs=P("gx", "gy", None), check_vma=False
    )
```

profile of v0, /device:TPU:1, one launch (start us, length us, event | category | flops | bytes accessed | tf_op | source)
XLA Modules:
  0.0 1415.3 jit_solution(11140029954902376108)
XLA Ops:
  0.8 4.9 collective-permute-start.1
  5.7 5.1 collective-permute-start
  28.2 4.0 collective-permute-start.7
  45.0 4.5 collective-permute-start.11
  54.6 5.2 collective-permute-done.14
  59.9 5.1 collective-permute-start.17
  71.3 6.6 collective-permute-start.19
  87.9 4.5 collective-permute-start.23
  98.9 4.0 collective-permute-start.27
  104.9 5.5 collective-permute-start.30
  113.0 7.0 collective-permute-start.31
  121.4 123.6 %all-reduce.17 = (f32[]{:T(128)}, f32[]{:T(128)}) all-reduce(f32[]{:T(128)} %get-tuple-element.100, f32[]{:T(128)} %get-tuple-element.25), channel_id=1, replica_groups=mesh['gx'=32,'gy'=16] {'gx','gy'}, use_global_device_ids=true, to_apply=%region_6.7 | all-reduce | flops 2 | bytes 16 | tf_op jit(solution)/shard_map/psum | solution.py:97
  247.0 100.5 %psum.86 = f32[]{:T(128)} all-reduce(f32[]{:T(128)} %multiply_reduce_fusion.9), channel_id=1, replica_groups=mesh['gx'=32,'gy'=16] {'gx','gy'}, use_global_device_ids=true, to_apply=%region_14.15 | all-reduce | flops 1 | bytes 8 | tf_op jit(solution)/shard_map/psum | solution.py:97
  357.2 4.0 collective-permute-start.35
  362.5 105.4 %psum.87 = f32[]{:T(128)} all-reduce(f32[]{:T(128)} %get-tuple-element.23), channel_id=1, replica_groups=mesh['gx'=32,'gy'=16] {'gx','gy'}, use_global_device_ids=true, to_apply=%region_16.17 | all-reduce | flops 1 | bytes 8 | tf_op jit(solution)/shard_map/psum | solution.py:119
  469.8 98.8 %psum.88 = f32[]{:T(128)} all-reduce(f32[]{:T(128)} %get-tuple-element.21), channel_id=1, replica_groups=mesh['gx'=32,'gy'=16] {'gx','gy'}, use_global_device_ids=true, to_apply=%region_18.19 | all-reduce | flops 1 | bytes 8 | tf_op jit(solution)/shard_map/psum | solution.py:97
  569.9 4.2 collective-permute-start.37
  585.7 103.7 %psum.89 = f32[]{:T(128)} all-reduce(f32[]{:T(128)} %get-tuple-element.19), channel_id=1, replica_groups=mesh['gx'=32,'gy'=16] {'gx','gy'}, use_global_device_ids=true, to_apply=%region_20.21 | all-reduce | flops 1 | bytes 8 | tf_op jit(solution)/shard_map/psum | solution.py:119
  691.3 99.4 %psum.90 = f32[]{:T(128)} all-reduce(f32[]{:T(128)} %get-tuple-element.17), channel_id=1, replica_groups=mesh['gx'=32,'gy'=16] {'gx','gy'}, use_global_device_ids=true, to_apply=%region_22.23 | all-reduce | flops 1 | bytes 8 | tf_op jit(solution)/shard_map/psum | solution.py:97
  792.1 4.2 collective-permute-start.41
  807.9 103.4 %psum.91 = f32[]{:T(128)} all-reduce(f32[]{:T(128)} %get-tuple-element.15), channel_id=1, replica_groups=mesh['gx'=32,'gy'=16] {'gx','gy'}, use_global_device_ids=true, to_apply=%region_24.25 | all-reduce | flops 1 | bytes 8 | tf_op jit(solution)/shard_map/psum | solution.py:119
  913.4 99.5 %psum.92 = f32[]{:T(128)} all-reduce(f32[]{:T(128)} %get-tuple-element.13), channel_id=1, replica_groups=mesh['gx'=32,'gy'=16] {'gx','gy'}, use_global_device_ids=true, to_apply=%region_26.27 | all-reduce | flops 1 | bytes 8 | tf_op jit(solution)/shard_map/psum | solution.py:97
  1014.2 4.2 collective-permute-start.45
  1024.7 4.0 collective-permute-start.47
  1030.1 103.4 %psum.93 = f32[]{:T(128)} all-reduce(f32[]{:T(128)} %get-tuple-element.11), channel_id=1, replica_groups=mesh['gx'=32,'gy'=16] {'gx','gy'}, use_global_device_ids=true, to_apply=%region_28.29 | all-reduce | flops 1 | bytes 8 | tf_op jit(solution)/shard_map/psum | solution.py:119
  1135.5 99.4 %psum.94 = f32[]{:T(128)} all-reduce(f32[]{:T(128)} %multiply_reduce_fusion.1), channel_id=1, replica_groups=mesh['gx'=32,'gy'=16] {'gx','gy'}, use_global_device_ids=true, to_apply=%region_30.31 | all-reduce | flops 1 | bytes 8 | tf_op jit(solution)/shard_map/psum | solution.py:97
  1236.1 4.2 collective-permute-start.49
  1252.0 103.5 %psum.95 = f32[]{:T(128)} all-reduce(f32[]{:T(128)} %fusion.238), channel_id=1, replica_groups=mesh['gx'=32,'gy'=16] {'gx','gy'}, use_global_device_ids=true, to_apply=%region_32.33 | all-reduce | flops 1 | bytes 8 | tf_op jit(solution)/shard_map/psum | solution.py:119
  1366.0 4.0 collective-permute-start.55
  1380.2 4.5 collective-permute-start.59
  1394.8 4.5 collective-permute-start.63
  1409.3 4.5 collective-permute-start.67
  (192 shorter events, 160.0 us)
Async XLA Ops:
  0.8 10.1 collective-permute-start.1
  5.7 6.0 collective-permute-start
  26.9 5.3 collective-permute-start.6
  33.1 10.7 collective-permute-start.9
  36.1 7.6 collective-permute-start.8
  38.1 11.5 collective-permute-start.13
  41.7 7.9 collective-permute-start.12
  43.7 10.6 collective-permute-start.10
  45.0 9.4 collective-permute-start.11
  53.1 6.7 collective-permute-start.14
  59.9 7.0 collective-permute-start.17
  70.0 7.9 collective-permute-start.18
  71.3 7.4 collective-permute-start.19
  86.6 11.6 collective-permute-start.22
  87.9 10.3 collective-permute-start.23
  92.5 12.4 collective-permute-start.26
  96.3 8.6 collective-permute-start.24
  98.9 12.8 collective-permute-start.27
  103.0 8.7 collective-permute-start.25
  104.9 15.1 %collective-permute-start.30 = (f32[3,1,128]{2,1,0:T(1,128)S(1)}, f32[3,1,128]{2,1,0:T(1,128)S(1)}, u32[]{:S(2)}, u32[]{:S(2)}) collective-permute-start(f32[3,1,128]{2,1,0:T(1,128)S(1)} %get-tuple-element.96), channel_id=1, source_target_pairs={{0,1},{1,2},{2,3},{3,4},{4,5},{5,6},{6,7},{7,8},{8,9},{9,10},{10,1... | collective-permute-start | bytes 4616 | tf_op jit(solution)/shard_map/ppermute | solution.py:21
  110.4 9.7 collective-permute-start.28
  111.7 8.4 collective-permute-start.29
  113.0 7.7 collective-permute-start.31
  355.9 5.3 collective-permute-start.34
  569.9 6.2 collective-permute-start.37
  792.1 6.2 collective-permute-start.41
  1014.2 6.2 collective-permute-start.45
  1023.4 5.3 collective-permute-start.46
  1236.1 6.2 collective-permute-start.49
  1378.9 5.8 collective-permute-start.58
  1393.5 5.8 collective-permute-start.62
  1408.0 5.8 collective-permute-start.66
  (39 other events, 202.5 us)
where the time goes:
time: 1430 us; the launch traced here: 1420 us
  blocking collectives  1140 us (80%)
  starting transfers between devices  195 us (14%)
  waiting for transfers between devices  53.8 us (4%)
  between operations  15.6 us (1%)
    psum x6, blocking collectives, squares(): return lax.psum(jnp.sum(residual * residual), ('gx', 'gy'))  621 us
    psum x5, blocking collectives, on_device(): alpha = norm_now / lax.psum(jnp.sum(direction * image), ('gx', 'gy'))  519 us
    ppermute x34, starting transfers between devices, extended(): lax.ppermute(lax.slice_in_dim(block, block.shape[dim] - width, None, axis...  137 us
    ppermute x34, starting transfers between devices, extended(): lax.ppermute(lax.slice_in_dim(block, 0, width, axis=dim), axis, backward)  57.9 us
    ppermute x34, waiting for transfers between devices, extended(): lax.ppermute(lax.slice_in_dim(block, 0, width, axis=dim), axis, backward)  45.3 us
  transfers between devices with their start and end apart: 68, of which 27 were waited for; matrix products, arithmetic and copies ran while one was open for 0% of the time, Pallas kernels for 0%

commit v1 on v0

v1 whole, which is shorter than its diff:
```python
import functools

import jax
import jax.numpy as jnp
from jax import lax
from jax.experimental import pallas as pl
from jax.experimental.pallas import tpu as pltpu
from jax.sharding import PartitionSpec as P

MESH = pl.DeviceIdType.MESH
ITERS = 6
FIRST = 1.0 / 1.2
CARRY = 2.0 / 7.0
SECOND = 0.75 / 0.7
KEEP = 1.0 + CARRY + SECOND * (1.0 - FIRST) / FIRST
VERTICAL = 1.0 / 16.0
PLANE_SCALES = (1.0, 0.25, 0.0625)
EDGE = 16
SPLIT = 4097.0

PAIRS = [(i, j) for i in range(ITERS) for j in range(i, ITERS)] + [(ITERS - 1, ITERS)]
SLOT = {pair: n for n, pair in enumerate(PAIRS)}
ROWS = 24


def two_sum(a, b):
    s = a + b
    t = s - a
    return s, (a - (s - t)) + (b - t)


def fast_two_sum(a, b):
    s = a + b
    return s, b - (s - a)


def halves(a):
    t = SPLIT * a
    high = t - (t - a)
    return high, a - high


def two_prod(a, b, a_halves=None, b_halves=None):
    ah, al = halves(a) if a_halves is None else a_halves
    bh, bl = halves(b) if b_halves is None else b_halves
    p = a * b
    return p, ((ah * bh - p) + ah * bl + al * bh) + al * bl


def dd_add(a, b):
    s, t = two_sum(a[0], b[0])
    return fast_two_sum(s, t + (a[1] + b[1]))


def dd_mul(a, b):
    p, t = two_prod(a[0], b[0])
    return fast_two_sum(p, t + (a[0] * b[1] + a[1] * b[0]))


def dd_neg(a):
    return -a[0], -a[1]


def dd_half(a):
    return 0.5 * a[0], 0.5 * a[1]


def dd_div(a, b):
    q = a[0] / b[0]
    p, t = two_prod(q, b[0])
    rest = ((a[0] - p) - t) + (a[1] - q * b[1])
    return fast_two_sum(q, rest / b[0])


def dd_dot(us, ws):
    terms = [dd_mul(u, w) for u, w in zip(us, ws)]
    while len(terms) > 1:
        terms = [dd_add(terms[i], terms[i + 1]) if i + 1 < len(terms) else terms[i] for i in range(0, len(terms), 2)]
    return terms[0]


def gradient_coefficients(gram):
    one = (jnp.ones_like(gram(0, 0)[0]), jnp.zeros_like(gram(0, 0)[0]))
    residual, direction, answer = [one], [one], [None] * ITERS
    norm_now = gram(0, 0)
    for turn in range(ITERS):
        image = []
        for k in range(turn + 2):
            terms = [direction[k]] if k <= turn else []
            if k >= 1:
                terms.append(direction[0] if k == 1 else dd_half(direction[k - 1]))
            if k + 1 <= turn:
                terms.append(dd_half(direction[k + 1]))
            total = terms[0]
            for term in terms[1:]:
                total = dd_add(total, term)
            image.append(total)
        along = dd_mul(direction[turn], dd_dot(image, [gram(i, turn) for i in range(turn + 2)]))
        alpha = dd_div(norm_now, along)
        for k in range(turn + 1):
            step = dd_mul(alpha, direction[k])
            answer[k] = step if answer[k] is None else dd_add(answer[k], step)
        if turn + 1 == ITERS:
            break
        less = dd_neg(alpha)
        steps = [dd_mul(less, value) for value in image]
        residual = [dd_add(residual[k], steps[k]) if k <= turn else steps[k] for k in range(turn + 2)]
        norm_next = dd_mul(residual[turn + 1], dd_dot(residual, [gram(i, turn + 1) for i in range(turn + 2)]))
        beta = dd_div(norm_next, norm_now)
        norm_now = norm_next
        direction = [dd_add(residual[k], dd_mul(beta, direction[k])) if k <= turn else residual[k] for k in range(turn + 2)]
    return [value[0] + value[1] for value in answer]


def loop(low, high, body):
    def step(p, carry):
        body(p)
        return carry

    lax.fori_loop(low, high, step, 0)


def lane_of(shape):
    return lax.broadcasted_iota(jnp.int32, shape, len(shape) - 1)


def box(reach, width):
    return [(i, j) for i in range(-reach, reach + 1) for j in range(-width, width + 1) if (i, j) != (0, 0)]


def ring(count, size):
    far = sorted(range(1, count), key=lambda d: -min(d, count - d))
    return [((d, 0) if size else (0, d)) for d in far]


def windows(offsets, count, rows, first, reach):
    out = []
    for dx, dy in sorted(offsets, key=lambda o: -abs(o[0]) - abs(o[1])):
        if dx == 0:
            start, planes, target = 0, count, first
        elif dx > 0:
            start = max(0, dx * count - reach)
            planes, target = count - start, first - dx * count + start
        else:
            start, planes = 0, min(count, reach + (dx + 1) * count)
            target = first - dx * count
        row, high, to = (EDGE, rows, EDGE) if dy == 0 else (EDGE + rows - 8, 8, EDGE - 8) if dy > 0 else (EDGE, 8, EDGE + rows)
        out.append((dx, dy, first + start, target, planes, row, to, high))
    return out


def tiles_of(geometry, fields):
    return sum(fields * w[4] * w[7] // 8 for w in geometry)


def kernel(
    counts, source, beta, shift, out,
    fields, coarse2, coarse3, rhs2, rhs3,
    masked1, wx1, wy1, wz1, diag1, inv1, step1, near1, iter1, start1,
    masked2, wx2, wy2, wz2, diag2, inv2, step2, near2, iter2, start2, sum2,
    masked3, wx3, wy3, wz3, own3, inside3, basis, sol3,
    pair_high, pair_low, bound_y, bound_x, gram_y, gram_x, scalars, dummy,
    load_sem, send_sem, recv_sem,
):
    nx, ny = counts
    gx, gy = lax.axis_index("gx"), lax.axis_index("gy")

    def device(dx, dy):
        return lax.rem(gx + (dx + nx), nx), lax.rem(gy + (dy + ny), ny)

    near, wide, far = box(1, 1), box(2, 1), box(7, 1)
    over_y, over_x = ring(ny, 0), ring(nx, 1)

    loads = [
        pltpu.make_async_copy(ref, fields.at[n, pl.ds(3, 4), pl.ds(EDGE, 32)], load_sem.at[n])
        for n, ref in enumerate((source, shift, beta))
    ]
    for load in loads:
        load.start()

    partners = sorted({((dx + nx) % nx, (dy + ny) % ny) for dx, dy in far + over_y + over_x})
    barrier = pltpu.get_barrier_semaphore()
    for dx, dy in partners:
        pl.semaphore_signal(barrier, 1, device_id=device(-dx, -dy), device_id_type=MESH)

    def send(phase, ref, geometry, stacked):
        for dx, dy, plane, target, planes, row, to, high in geometry:
            here, there = (pl.ds(plane, planes), pl.ds(row, high)), (pl.ds(target, planes), pl.ds(to, high))
            if stacked:
                here, there = (slice(None), *here), (slice(None), *there)
            pltpu.make_async_remote_copy(
                src_ref=ref.at[here], dst_ref=ref.at[there], send_sem=send_sem.at[phase], recv_sem=recv_sem.at[phase],
                device_id=device(dx, dy), device_id_type=MESH,
            ).start()

    def wait(sems, phase, tiles):
        part = dummy.at[pl.ds(0, tiles)]
        pltpu.make_async_copy(part, part, sems.at[phase]).wait()

    def spread(phase, ref, offsets):
        for dx, dy in offsets:
            pltpu.make_async_remote_copy(
                src_ref=ref.at[0], dst_ref=ref.at[max(dx, dy)], send_sem=send_sem.at[phase], recv_sem=recv_sem.at[phase],
                device_id=device(dx, dy), device_id_type=MESH,
            ).start()

    def wait_spread(sems, phase, ref, count):
        part = ref.at[pl.ds(1, count - 1)]
        pltpu.make_async_copy(part, part, sems.at[phase]).wait()

    def inside(p, rows, low, first, count, own_planes, own_rows):
        plane = gx * own_planes + (p - first)
        row = gy * own_rows + (low - EDGE) + lax.broadcasted_iota(jnp.int32, (rows, 128), 0)
        fits = jnp.logical_and(plane >= 0, plane < nx * own_planes).astype(jnp.int32)
        return jnp.where(jnp.logical_and(row >= 0, row < ny * own_rows), fits, 0) > 0

    def off(v, wx, wy, wz, p, low, rows):
        here = v[p, pl.ds(low, rows), :]
        up = wz[p, pl.ds(low, rows), :]
        total = wx[p, pl.ds(low, rows), :] * v[p + 1, pl.ds(low, rows), :]
        total = total + wx[p - 1, pl.ds(low, rows), :] * v[p - 1, pl.ds(low, rows), :]
        total = total + wy[p, pl.ds(low, rows), :] * v[p, pl.ds(low + 1, rows), :]
        total = total + wy[p, pl.ds(low - 1, rows), :] * v[p, pl.ds(low - 1, rows), :]
        total = total + up * pltpu.roll(here, 127, 1)
        return total + pltpu.roll(up * here, 1, 1)

    def weights(b, p, low, rows, plane, upright):
        here = b[p, pl.ds(low, rows), :]
        lane = lane_of((rows, 128))
        wxp = plane * (here + b[p + 1, pl.ds(low, rows), :])
        wxm = plane * (here + b[p - 1, pl.ds(low, rows), :])
        wyp = plane * (here + b[p, pl.ds(low + 1, rows), :])
        wym = plane * (here + b[p, pl.ds(low - 1, rows), :])
        wzp = upright * (here + jnp.where(lane < 127, pltpu.roll(here, 127, 1), 0.0))
        wzm = upright * (here + jnp.where(lane > 0, pltpu.roll(here, 1, 1), 0.0))
        return wxp, wyp, jnp.where(lane < 127, wzp, 0.0), wxp + wxm + wyp + wym + wzp + wzm

    def prepare(refs, pair, rows, first, own, scale):
        masked, wx, wy, wz, diag, inv = refs
        shift_at, beta_at = pair

        def clean(p):
            ok = inside(p, rows, 8, first, 10, own[0], own[1])
            masked[p, pl.ds(8, rows), :] = jnp.where(ok, beta_at(p), 0.0)

        def fill(p):
            wxp, wyp, wzp, total = weights(masked, p, 8, rows, 0.5 * scale, 0.5 * VERTICAL)
            total = total + shift_at(p)
            wx[p, pl.ds(8, rows), :] = wxp
            wy[p, pl.ds(8, rows), :] = wyp
            wz[p, pl.ds(8, rows), :] = wzp
            diag[p, pl.ds(8, rows), :] = total
            ok = inside(p, rows, 8, first, 10, own[0], own[1])
            inv[p, pl.ds(8, rows), :] = jnp.where(ok, 1.0 / total, 0.0)

        loop(0, 10, clean)
        loop(1, 9, fill)

    def coarsen_rows(ref, at, rows):
        even = ref[at, pl.ds(EDGE, rows // 2, stride=2), :]
        return 0.25 * (even + ref[at, pl.ds(EDGE + 1, rows // 2, stride=2), :])

    for load in loads:
        load.wait()
    for n, level in ((0, 1), (1, 2)):
        for q in range(2):
            both = fields[1 + n, 3 + 2 * q, pl.ds(EDGE, 32), :] + fields[1 + n, 4 + 2 * q, pl.ds(EDGE, 32), :]
            near1[q, pl.ds(EDGE, 32), :] = both
            coarse2[n, 4 + q, pl.ds(EDGE, 16), :] = coarsen_rows(near1, q, 32)
        near2[0, pl.ds(EDGE, 16), :] = coarse2[n, 4, pl.ds(EDGE, 16), :] + coarse2[n, 5, pl.ds(EDGE, 16), :]
        coarse3[n, 7, pl.ds(EDGE, 8), :] = coarsen_rows(near2, 0, 16)
    shift_own, beta_own = coarse3[0, 7, pl.ds(EDGE, 8), :], coarse3[1, 7, pl.ds(EDGE, 8), :]
    around = pltpu.roll(beta_own, 1, 0) + pltpu.roll(beta_own, 7, 0) + pltpu.roll(beta_own, 1, 1) + pltpu.roll(beta_own, 127, 1)
    bound = jnp.max(shift_own + PLANE_SCALES[2] * (6.0 * beta_own + 1.5 * around))
    bound_y[0] = jnp.full((1, 128), bound, jnp.float32)

    pl.semaphore_wait(barrier, len(partners))
    geo_fields = windows(near, 4, 32, 3, 3)
    geo_coarse2 = windows(wide, 2, 16, 4, 4)
    geo_coarse3 = windows(far, 1, 8, 7, 7)
    geo_iter1 = windows(near, 4, 32, 3, 2)
    geo_rhs2 = windows(near, 2, 16, 4, 2)
    send(0, fields, geo_fields, True)
    send(1, coarse2, geo_coarse2, True)
    spread(7, bound_y, over_y)
    send(2, coarse3, geo_coarse3, True)

    wait(recv_sem, 0, tiles_of(geo_fields, 3))
    level1 = (masked1, wx1, wy1, wz1, diag1, inv1)
    prepare(
        level1, (lambda p: fields[1, p, pl.ds(8, 48), :], lambda p: fields[2, p, pl.ds(8, 48), :]), 48, 3, (4, 32), PLANE_SCALES[0]
    )

    def first_step(step, inv, value, rows):
        def body(p):
            step[p, pl.ds(8, rows), :] = FIRST * value(p) * inv[p, pl.ds(8, rows), :]

        return body

    def smooth(step, wx, wy, wz, inv, p, low, rows):
        part = off(step, wx, wy, wz, p, low, rows)
        return KEEP * step[p, pl.ds(low, rows), :] + SECOND * inv[p, pl.ds(low, rows), :] * part

    loop(1, 9, first_step(step1, inv1, lambda p: fields[0, p, pl.ds(8, 48), :], 48))

    def presmooth1(p):
        near1[p, pl.ds(8, 48), :] = smooth(step1, wx1, wy1, wz1, inv1, p, 8, 48)

    loop(2, 8, presmooth1)

    def residual(f, v, level, p, low, rows):
        _, wx, wy, wz, diag, _ = level
        value = f(p, low, rows) - diag[p, pl.ds(low, rows), :] * v[p, pl.ds(low, rows), :]
        return value + off(v, wx, wy, wz, p, low, rows)

    def source_at(p, low, rows):
        return fields[0, p, pl.ds(low, rows), :]

    def rhs2_at(p, low, rows):
        return rhs2[p, pl.ds(low, rows), :]

    def restrict1(q):
        both = residual(source_at, near1, level1, 3 + 2 * q, EDGE, 32) + residual(source_at, near1, level1, 4 + 2 * q, EDGE, 32)
        start1[q, pl.ds(EDGE, 32), :] = both
        rhs2[4 + q, pl.ds(EDGE, 16), :] = coarsen_rows(start1, q, 32)

    loop(0, 2, restrict1)
    send(3, rhs2, geo_rhs2, False)

    def keep1(p):
        iter1[p, pl.ds(EDGE, 32), :] = near1[p, pl.ds(EDGE, 32), :]

    loop(3, 7, keep1)
    send(4, iter1, geo_iter1, False)

    wait(recv_sem, 1, tiles_of(geo_coarse2, 2))
    level2 = (masked2, wx2, wy2, wz2, diag2, inv2)
    prepare(
        level2, (lambda p: coarse2[0, p, pl.ds(8, 32), :], lambda p: coarse2[1, p, pl.ds(8, 32), :]), 32, 4, (2, 16), PLANE_SCALES[1]
    )
    wait_spread(recv_sem, 7, bound_y, ny)
    bound_x[0] = functools.reduce(jnp.maximum, [bound_y[n] for n in range(ny)])
    spread(8, bound_x, over_x)

    wait(recv_sem, 3, tiles_of(geo_rhs2, 1))
    loop(2, 8, first_step(step2, inv2, lambda p: rhs2_at(p, 8, 32), 32))

    def presmooth2(p):
        near2[p, pl.ds(8, 32), :] = smooth(step2, wx2, wy2, wz2, inv2, p, 8, 32)

    loop(3, 7, presmooth2)
    both = residual(rhs2_at, near2, level2, 4, EDGE, 16) + residual(rhs2_at, near2, level2, 5, EDGE, 16)
    start2[0, pl.ds(EDGE, 16), :] = both
    rhs3[7, pl.ds(EDGE, 8), :] = coarsen_rows(start2, 0, 16)
    send(5, rhs3, geo_coarse3, False)
    for p in (4, 5):
        iter2[p, pl.ds(EDGE, 16), :] = near2[p, pl.ds(EDGE, 16), :]
    send(6, iter2, geo_coarse2, False)

    wait(recv_sem, 2, tiles_of(geo_coarse3, 2))
    wait_spread(recv_sem, 8, bound_x, nx)
    scale = 2.0 / functools.reduce(jnp.maximum, [bound_x[n] for n in range(nx)])

    def clean3(p):
        ok = inside(p, 24, 8, 7, 15, 1, 8)
        masked3[p, pl.ds(8, 24), :] = jnp.where(ok, coarse3[1, p, pl.ds(8, 24), :], 0.0)

    loop(0, 15, clean3)
    wx3[0, pl.ds(8, 24), :] = (PLANE_SCALES[2] * scale) * (masked3[0, pl.ds(8, 24), :] + masked3[1, pl.ds(8, 24), :])

    def fill3(p):
        wxp, wyp, wzp, total = weights(masked3, p, 8, 24, PLANE_SCALES[2] * scale, VERTICAL * scale)
        total = total + 2.0 * scale * coarse3[0, p, pl.ds(8, 24), :]
        wx3[p, pl.ds(8, 24), :] = wxp
        wy3[p, pl.ds(8, 24), :] = wyp
        wz3[p, pl.ds(8, 24), :] = wzp
        ok = inside(p, 24, 8, 7, 15, 1, 8)
        own3[p, pl.ds(8, 24), :] = jnp.where(ok, total - 2.0, 0.0)
        inside3[p, pl.ds(8, 24), :] = jnp.where(ok, 1.0, 0.0)

    loop(1, 14, fill3)
    wait(recv_sem, 5, tiles_of(geo_coarse3, 1))

    def begin3(p):
        ok = inside(p, 24, 8, 7, 15, 1, 8)
        basis[0, p, pl.ds(8, 24), :] = jnp.where(ok, rhs3[p, pl.ds(8, 24), :], 0.0)

    loop(0, 15, begin3)

    def doubled(v, p, low, rows):
        value = own3[p, pl.ds(low, rows), :] * v[p, pl.ds(low, rows), :]
        return value - inside3[p, pl.ds(low, rows), :] * off(v, wx3, wy3, wz3, p, low, rows)

    for k in range(ITERS):
        low, rows, reach = (8, 24, 6 - k) if k < ITERS - 1 else (EDGE, 8, 0)

        def advance(p, k=k, low=low, rows=rows):
            value = doubled(basis.at[k], p, low, rows)
            value = 0.5 * value if k == 0 else value - basis[k - 1, p, pl.ds(low, rows), :]
            basis[k + 1, p, pl.ds(low, rows), :] = value

        loop(7 - reach, 8 + reach, advance)

    own = [basis[k, 7, pl.ds(EDGE, 8), :] for k in range(ITERS + 1)]
    parts = [halves(v) for v in own]
    for n, (i, j) in enumerate(PAIRS):
        high, low = two_prod(own[i], own[j], parts[i], parts[j])
        pair_high[pl.ds(8 * n, 8), :] = high
        pair_low[pl.ds(8 * n, 8), :] = low
    for n in range(len(PAIRS), ROWS):
        pair_high[pl.ds(8 * n, 8), :] = jnp.zeros((8, 128), jnp.float32)
        pair_low[pl.ds(8 * n, 8), :] = jnp.zeros((8, 128), jnp.float32)

    def merge(a, b):
        s, t = two_sum(a[0], b[0])
        return s, t + (a[1] + b[1])

    def tree(terms):
        while len(terms) > 1:
            terms = [merge(terms[i], terms[i + 1]) if i + 1 < len(terms) else terms[i] for i in range(0, len(terms), 2)]
        return terms[0]

    sums = tree([(pair_high[pl.ds(s, ROWS, stride=8), :], pair_low[pl.ds(s, ROWS, stride=8), :]) for s in range(8)])
    for d in (64, 32, 16, 8, 4, 2, 1):
        sums = merge(sums, (pltpu.roll(sums[0], d, 1), pltpu.roll(sums[1], d, 1)))
    lane, row = lane_of((ROWS, 128)), lax.broadcasted_iota(jnp.int32, (ROWS, 128), 0)
    line = jnp.where(lane == row, sums[0], jnp.where(lane == row + 64, sums[1], 0.0))
    gram_y[0] = jnp.sum(line, axis=0, keepdims=True)

    def total_of(ref, count):
        zero = jnp.zeros((1, 128), jnp.float32)
        s, t = tree([(ref[n], zero) for n in range(count)])
        return s + jnp.where(lane_of((1, 128)) >= 64, pltpu.roll(t, 64, 1), 0.0)

    spread(9, gram_y, over_y)
    wait_spread(recv_sem, 9, gram_y, ny)
    gram_x[0] = total_of(gram_y, ny)
    spread(10, gram_x, over_x)
    wait(recv_sem, 4, tiles_of(geo_iter1, 1))
    wait(recv_sem, 6, tiles_of(geo_coarse2, 1))
    wait_spread(recv_sem, 10, gram_x, nx)
    entries = jnp.broadcast_to(total_of(gram_x, nx), (2 * ROWS, 128))
    lane, row = lane_of((2 * ROWS, 128)), lax.broadcasted_iota(jnp.int32, (2 * ROWS, 128), 0)
    place = jnp.where(row < ROWS, row, row + (64 - ROWS))
    column = jnp.sum(jnp.where(lane == place, entries, 0.0), axis=1, keepdims=True)
    scalars[...] = jnp.broadcast_to(column, (2 * ROWS, 128))

    def gram(i, j):
        n = SLOT[(min(i, j), max(i, j))]
        return scalars[pl.ds(n, 1), :], scalars[pl.ds(ROWS + n, 1), :]

    answer = [value * scale for value in gradient_coefficients(gram)]

    for n in range(5):
        p = 5 + n
        total = answer[0] * basis[0, p, pl.ds(8, 24), :]
        for k in range(1, ITERS):
            total = total + answer[k] * basis[k, p, pl.ds(8, 24), :]
        sol3[n, pl.ds(8, 24), :] = total

    def prolong2(p):
        value = sol3[p // 2, pl.ds(12, 16), :]
        start2[p, pl.ds(8, 16, stride=2), :] = value
        start2[p, pl.ds(9, 16, stride=2), :] = value
        ok = inside(p, 32, 8, 4, 10, 2, 16)
        start2[p, pl.ds(8, 32), :] = jnp.where(ok, start2[p, pl.ds(8, 32), :] + iter2[p, pl.ds(8, 32), :], 0.0)

    loop(1, 9, prolong2)
    loop(2, 8, first_step(step2, inv2, lambda p: residual(rhs2_at, start2, level2, p, 8, 32), 32))

    def post2(p):
        sum2[p, pl.ds(8, 32), :] = start2[p, pl.ds(8, 32), :] + smooth(step2, wx2, wy2, wz2, inv2, p, 8, 32)

    loop(3, 7, post2)

    def prolong1(p):
        value = sum2[(p + 5) // 2, pl.ds(12, 24), :]
        start1[p, pl.ds(8, 24, stride=2), :] = value
        start1[p, pl.ds(9, 24, stride=2), :] = value
        ok = inside(p, 48, 8, 3, 10, 4, 32)
        start1[p, pl.ds(8, 48), :] = jnp.where(ok, start1[p, pl.ds(8, 48), :] + iter1[p, pl.ds(8, 48), :], 0.0)

    loop(1, 9, prolong1)
    loop(2, 8, first_step(step1, inv1, lambda p: residual(source_at, start1, level1, p, 8, 48), 48))

    def post1(p):
        out[p - 3] = start1[p, pl.ds(EDGE, 32), :] + smooth(step1, wx1, wy1, wz1, inv1, p, EDGE, 32)

    loop(3, 7, post1)

    wait(send_sem, 0, tiles_of(geo_fields, 3))
    wait(send_sem, 1, tiles_of(geo_coarse2, 2))
    wait(send_sem, 2, tiles_of(geo_coarse3, 2))
    wait(send_sem, 3, tiles_of(geo_rhs2, 1))
    wait(send_sem, 4, tiles_of(geo_iter1, 1))
    wait(send_sem, 5, tiles_of(geo_coarse3, 1))
    wait(send_sem, 6, tiles_of(geo_coarse2, 1))
    wait_spread(send_sem, 7, bound_y, ny)
    wait_spread(send_sem, 8, bound_x, nx)
    wait_spread(send_sem, 9, gram_y, ny)
    wait_spread(send_sem, 10, gram_x, nx)


def solution(mesh):
    nx, ny = mesh.shape["gx"], mesh.shape["gy"]

    def vmem(*shape):
        return pltpu.VMEM(shape, jnp.float32)

    one = [vmem(10, 64, 128)] * 10
    two = [vmem(10, 48, 128)] * 11
    three = [vmem(15, 40, 128)] * 6 + [vmem(ITERS + 1, 15, 40, 128), vmem(5, 40, 128)]

    def on_device(source, beta, shift):
        return pl.pallas_call(
            functools.partial(kernel, (nx, ny)),
            out_shape=jax.ShapeDtypeStruct(source.shape, jnp.float32),
            in_specs=[pl.BlockSpec(memory_space=pl.ANY)] * 3,
            out_specs=pl.BlockSpec(memory_space=pltpu.VMEM),
            scratch_shapes=[
                vmem(3, 10, 64, 128), vmem(2, 10, 48, 128), vmem(2, 15, 40, 128), vmem(10, 48, 128), vmem(15, 40, 128),
                *one, *two, *three,
                vmem(8 * ROWS, 128), vmem(8 * ROWS, 128),
                vmem(ny, 1, 128), vmem(nx, 1, 128), vmem(ny, 1, 128), vmem(nx, 1, 128),
                vmem(2 * ROWS, 128), vmem(140, 8, 128),
                pltpu.SemaphoreType.DMA((3,)), pltpu.SemaphoreType.DMA((11,)), pltpu.SemaphoreType.DMA((11,)),
            ],
            compiler_params=pltpu.CompilerParams(collective_id=0, has_side_effects=True, vmem_limit_bytes=40 * 2**20),
        )(source, beta, shift)

    placed = P("gx", "gy", None)
    return jax.shard_map(on_device, mesh=mesh, in_specs=(placed,) * 3, out_specs=placed, check_vma=False)
```

time: 1430 us -> 64.9 us (0.05); the launches traced: 1420 us -> 64.7 us
  blocking collectives: 1140 us -> 0 us
  starting transfers between devices: 195 us -> 0 us
  Pallas kernels: 0 us -> 61.5 us
  waiting for transfers between devices: 53.8 us -> 0 us
  between operations: 15.6 us -> 0.01 us
    psum x11 -> x0, blocking collectives: 1140 us -> none  [the longest x6 621 us: squares(): return lax.psum(jnp.sum(residual * residual), ('gx', 'gy'))]
    ppermute x68 -> x0, starting transfers between devices: 195 us -> none  [the longest x34 137 us: extended(): lax.ppermute(lax.slice_in_dim(block, block.shape[dim] - width, None, axis...]
    pallas_call x0 -> x1, Pallas kernels: none -> 61.5 us  [on_device(): pl.pallas_call(functools.partial(kernel, (nx, ny)), out_shape=jax.ShapeDt...]
    ppermute x68 -> x0, waiting for transfers between devices: 53.8 us -> none  [the longest x34 45.3 us: extended(): lax.ppermute(lax.slice_in_dim(block, 0, width, axis=dim), axis, backward)]
  transfers between devices with their start and end apart: 68 -> 0, of which waited for: 27 -> 0; matrix products, arithmetic and copies ran while one was open for 0% -> 0% of each run, Pallas kernels for 0% -> 0%
where the time goes in v1:
time: 64.9 us; the launch traced here: 64.7 us
  Pallas kernels  61.5 us (95%)
  local copies, waits for them, and re-layouts  3.15 us (5%)
    pallas_call x1, Pallas kernels, on_device(): pl.pallas_call(functools.partial(kernel, (nx, ny)), out_shape=jax.ShapeDt...  61.5 us
    unnamed x7, local copies, waits for them, and re-layouts  3.15 us

profile of v1, /device:TPU:1, one launch (start us, length us, event | category | flops | bytes accessed | tf_op | source)
XLA Modules:
  0.0 64.7 jit_solution(11316620454634806751)
XLA Ops:
  0.0 0.0 copy-start
  0.0 0.8 %copy-done = f32[4,32,128]{2,1,0:T(8,128)S(1)} copy-done((f32[4,32,128]{2,1,0:T(8,128)S(1)}, f32[4,32,128]{2,1,0:T(8,128)}, u32[]{:S(2)}) %copy-start) | copy-done | bytes 65560
  0.8 0.0 copy-start.1
  0.8 0.8 %copy-done.1 = f32[4,32,128]{2,1,0:T(8,128)S(1)} copy-done((f32[4,32,128]{2,1,0:T(8,128)S(1)}, f32[4,32,128]{2,1,0:T(8,128)}, u32[]{:S(2)}) %copy-start.1) | copy-done | bytes 65560
  1.7 0.0 copy-start.2
  1.7 0.8 %copy-done.2 = f32[4,32,128]{2,1,0:T(8,128)S(1)} copy-done((f32[4,32,128]{2,1,0:T(8,128)S(1)}, f32[4,32,128]{2,1,0:T(8,128)}, u32[]{:S(2)}) %copy-start.2) | copy-done | bytes 65560
  2.5 61.5 %shard_map.37 = f32[4,32,128]{2,1,0:T(8,128)S(1)} custom-call(f32[4,32,128]{2,1,0:T(8,128)S(1)} %copy-done, f32[4,32,128]{2,1,0:T(8,128)S(1)} %copy-done.1, f32[4,32,128]{2,1,0:T(8,128)S(1)} %copy-done.2), custom_call_target="tpu_custom_call" | custom-call | tf_op jit(solution)/shard_map/pallas_call | solution.py:515
  64.1 0.6 copy.5
Async XLA Ops:
  0.0 0.8 %copy-start = (f32[4,32,128]{2,1,0:T(8,128)S(1)}, f32[4,32,128]{2,1,0:T(8,128)}, u32[]{:S(2)}) copy-start(f32[4,32,128]{2,1,0:T(8,128)} %source.1) | copy-start | bytes 196612
  0.8 0.8 %copy-start.1 = (f32[4,32,128]{2,1,0:T(8,128)S(1)}, f32[4,32,128]{2,1,0:T(8,128)}, u32[]{:S(2)}) copy-start(f32[4,32,128]{2,1,0:T(8,128)} %beta.1) | copy-start | bytes 196612
  1.7 0.8 %copy-start.2 = (f32[4,32,128]{2,1,0:T(8,128)S(1)}, f32[4,32,128]{2,1,0:T(8,128)}, u32[]{:S(2)}) copy-start(f32[4,32,128]{2,1,0:T(8,128)} %shift.1) | copy-start | bytes 196612

commit v2 on v1

--- a/solution.py
+++ b/solution.py
@@ -117,7 +117,8 @@
         body(p)
         return carry
 
-    lax.fori_loop(low, high, step, 0)
+    for p in range(low, high):
+        body(p)
 
 
 def lane_of(shape):
@@ -526,7 +527,7 @@
                 pltpu.SemaphoreType.DMA((3,)), pltpu.SemaphoreType.DMA((11,)), pltpu.SemaphoreType.DMA((11,)),
             ],
             compiler_params=pltpu.CompilerParams(collective_id=0, has_side_effects=True, vmem_limit_bytes=40 * 2**20),
-        )(source, beta, shift)
+        )(*[pltpu.with_memory_space_constraint(x, pltpu.HBM) for x in (source, beta, shift)])
 
     placed = P("gx", "gy", None)
     return jax.shard_map(on_device, mesh=mesh, in_specs=(placed,) * 3, out_specs=placed, check_vma=False)

time: 64.9 us -> 57.5 us (0.89)
  Pallas kernels: 61.5 us -> 56.7 us
  local copies, waits for them, and re-layouts: 3.15 us -> 0.63 us
    pallas_call x1, Pallas kernels: 61.5 us -> 56.7 us  [on_device(): pl.pallas_call(functools.partial(kernel, (nx, ny)), out_shape=jax.ShapeDt...]
    unnamed x7 -> x1, local copies, waits for them, and re-layouts: 3.15 us -> 0.63 us
where the time goes in v2:
time: 57.5 us; the launch traced here: 57.3 us
  Pallas kernels  56.7 us (99%)
  local copies, waits for them, and re-layouts  0.63 us (1%)
    pallas_call x1, Pallas kernels, on_device(): pl.pallas_call(functools.partial(kernel, (nx, ny)), out_shape=jax.ShapeDt...  56.7 us

profile of v2, /device:TPU:1, one launch (start us, length us, event | category | flops | bytes accessed | tf_op | source)
XLA Modules:
  0.0 57.3 jit_solution(10142134383032486667)
XLA Ops:
  0.0 56.7 %shard_map.37 = f32[4,32,128]{2,1,0:T(8,128)S(1)} custom-call(f32[4,32,128]{2,1,0:T(8,128)} %source.1, f32[4,32,128]{2,1,0:T(8,128)} %beta.1, f32[4,32,128]{2,1,0:T(8,128)} %shift.1), custom_call_target="tpu_custom_call" | custom-call | tf_op jit(solution)/shard_map/pallas_call | solution.py:516
  56.7 0.6 %copy.5 = f32[4,32,128]{2,1,0:T(8,128)} copy(f32[4,32,128]{2,1,0:T(8,128)S(1)} %shard_map.37) | data formatting | bytes 131072

commit v3 on v2

--- a/solution.py
+++ b/solution.py
@@ -160,7 +160,7 @@
     masked1, wx1, wy1, wz1, diag1, inv1, step1, near1, iter1, start1,
     masked2, wx2, wy2, wz2, diag2, inv2, step2, near2, iter2, start2, sum2,
     masked3, wx3, wy3, wz3, own3, inside3, basis, sol3,
-    pair_high, pair_low, bound_y, bound_x, gram_y, gram_x, scalars, dummy,
+    pair_high, pair_low, bound_y, few, more, last, gram_y, gram_x, scalars, dummy,
     load_sem, send_sem, recv_sem,
 ):
     nx, ny = counts
@@ -171,6 +171,10 @@
 
     near, wide, far = box(1, 1), box(2, 1), box(7, 1)
     over_y, over_x = ring(ny, 0), ring(nx, 1)
+    middle = [o for o in far if 3 <= abs(o[0]) <= 4]
+    outer = [o for o in far if abs(o[0]) > 4]
+    few_x = [(d, 0) for d in (4, -4, 3, -3, 2, -2, 1, -1)]
+    more_x, last_x = [(8, 0), (-8, 0)], [(nx // 2, 0)]
 
     loads = [
         pltpu.make_async_copy(ref, fields.at[n, pl.ds(3, 4), pl.ds(EDGE, 32)], load_sem.at[n])
@@ -179,7 +183,7 @@
     for load in loads:
         load.start()
 
-    partners = sorted({((dx + nx) % nx, (dy + ny) % ny) for dx, dy in far + over_y + over_x})
+    partners = sorted({(dx, dy % ny) for dx, dy in wide + over_y}, key=lambda o: abs(o[0]) + min(o[1], ny - o[1]))
     barrier = pltpu.get_barrier_semaphore()
     for dx, dy in partners:
         pl.semaphore_signal(barrier, 1, device_id=device(-dx, -dy), device_id_type=MESH)
@@ -198,10 +202,10 @@
         part = dummy.at[pl.ds(0, tiles)]
         pltpu.make_async_copy(part, part, sems.at[phase]).wait()
 
-    def spread(phase, ref, offsets):
-        for dx, dy in offsets:
+    def spread(phase, ref, offsets, slots=None):
+        for n, (dx, dy) in enumerate(offsets):
             pltpu.make_async_remote_copy(
-                src_ref=ref.at[0], dst_ref=ref.at[max(dx, dy)], send_sem=send_sem.at[phase], recv_sem=recv_sem.at[phase],
+                src_ref=ref.at[0], dst_ref=ref.at[max(dx, dy) if slots is None else 1 + n], send_sem=send_sem.at[phase], recv_sem=recv_sem.at[phase],
                 device_id=device(dx, dy), device_id_type=MESH,
             ).start()
 
@@ -261,8 +265,17 @@
         even = ref[at, pl.ds(EDGE, rows // 2, stride=2), :]
         return 0.25 * (even + ref[at, pl.ds(EDGE + 1, rows // 2, stride=2), :])
 
+    geo_fields = windows(near, 4, 32, 3, 3)
+    geo_coarse2 = windows(wide, 2, 16, 4, 3)
+    geo_coarse3, geo_middle3, geo_outer3 = (windows(part, 1, 8, 7, 7) for part in (wide, middle, outer))
+    geo_rhs3 = windows(far, 1, 8, 7, 7)
+    geo_iter1 = windows(near, 4, 32, 3, 2)
+    geo_rhs2 = windows(near, 2, 16, 4, 2)
     for load in loads:
         load.wait()
+    pl.semaphore_wait(barrier, len(partners))
+    send(0, fields, geo_fields, True)
+
     for n, level in ((0, 1), (1, 2)):
         for q in range(2):
             both = fields[1 + n, 3 + 2 * q, pl.ds(EDGE, 32), :] + fields[1 + n, 4 + 2 * q, pl.ds(EDGE, 32), :]
@@ -275,18 +288,16 @@
     bound = jnp.max(shift_own + PLANE_SCALES[2] * (6.0 * beta_own + 1.5 * around))
     bound_y[0] = jnp.full((1, 128), bound, jnp.float32)
 
-    pl.semaphore_wait(barrier, len(partners))
-    geo_fields = windows(near, 4, 32, 3, 3)
-    geo_coarse2 = windows(wide, 2, 16, 4, 4)
-    geo_coarse3 = windows(far, 1, 8, 7, 7)
-    geo_iter1 = windows(near, 4, 32, 3, 2)
-    geo_rhs2 = windows(near, 2, 16, 4, 2)
-    send(0, fields, geo_fields, True)
+    spread(7, bound_y, over_y)
     send(1, coarse2, geo_coarse2, True)
-    spread(7, bound_y, over_y)
     send(2, coarse3, geo_coarse3, True)
 
     wait(recv_sem, 0, tiles_of(geo_fields, 3))
+    wait(recv_sem, 1, tiles_of(geo_coarse2, 2))
+    wait_spread(recv_sem, 7, bound_y, ny)
+    few[0] = functools.reduce(jnp.maximum, [bound_y[n] for n in range(ny)])
+    spread(8, few, few_x, True)
+    send(11, coarse3, geo_middle3, True)
     level1 = (masked1, wx1, wy1, wz1, diag1, inv1)
     prepare(
         level1, (lambda p: fields[1, p, pl.ds(8, 48), :], lambda p: fields[2, p, pl.ds(8, 48), :]), 48, 3, (4, 32), PLANE_SCALES[0]
@@ -334,15 +345,14 @@
     loop(3, 7, keep1)
     send(4, iter1, geo_iter1, False)
 
-    wait(recv_sem, 1, tiles_of(geo_coarse2, 2))
     level2 = (masked2, wx2, wy2, wz2, diag2, inv2)
     prepare(
         level2, (lambda p: coarse2[0, p, pl.ds(8, 32), :], lambda p: coarse2[1, p, pl.ds(8, 32), :]), 32, 4, (2, 16), PLANE_SCALES[1]
     )
-    wait_spread(recv_sem, 7, bound_y, ny)
-    bound_x[0] = functools.reduce(jnp.maximum, [bound_y[n] for n in range(ny)])
-    spread(8, bound_x, over_x)
-
+    wait_spread(recv_sem, 8, few, 9)
+    more[0] = functools.reduce(jnp.maximum, [few[n] for n in range(9)])
+    spread(12, more, more_x, True)
+    send(13, coarse3, geo_outer3, True)
     wait(recv_sem, 3, tiles_of(geo_rhs2, 1))
     loop(2, 8, first_step(step2, inv2, lambda p: rhs2_at(p, 8, 32), 32))
 
@@ -353,14 +363,19 @@
     both = residual(rhs2_at, near2, level2, 4, EDGE, 16) + residual(rhs2_at, near2, level2, 5, EDGE, 16)
     start2[0, pl.ds(EDGE, 16), :] = both
     rhs3[7, pl.ds(EDGE, 8), :] = coarsen_rows(start2, 0, 16)
-    send(5, rhs3, geo_coarse3, False)
+    send(5, rhs3, geo_rhs3, False)
     for p in (4, 5):
         iter2[p, pl.ds(EDGE, 16), :] = near2[p, pl.ds(EDGE, 16), :]
     send(6, iter2, geo_coarse2, False)
 
+    wait_spread(recv_sem, 12, more, 3)
+    last[0] = functools.reduce(jnp.maximum, [more[n] for n in range(3)])
+    spread(14, last, last_x, True)
     wait(recv_sem, 2, tiles_of(geo_coarse3, 2))
-    wait_spread(recv_sem, 8, bound_x, nx)
-    scale = 2.0 / functools.reduce(jnp.maximum, [bound_x[n] for n in range(nx)])
+    wait(recv_sem, 11, tiles_of(geo_middle3, 2))
+    wait(recv_sem, 13, tiles_of(geo_outer3, 2))
+    wait_spread(recv_sem, 14, last, 2)
+    scale = 2.0 / jnp.maximum(last[0], last[1])
 
     def clean3(p):
         ok = inside(p, 24, 8, 7, 15, 1, 8)
@@ -380,7 +395,7 @@
         inside3[p, pl.ds(8, 24), :] = jnp.where(ok, 1.0, 0.0)
 
     loop(1, 14, fill3)
-    wait(recv_sem, 5, tiles_of(geo_coarse3, 1))
+    wait(recv_sem, 5, tiles_of(geo_rhs3, 1))
 
     def begin3(p):
         ok = inside(p, 24, 8, 7, 15, 1, 8)
@@ -492,12 +507,16 @@
     wait(send_sem, 0, tiles_of(geo_fields, 3))
     wait(send_sem, 1, tiles_of(geo_coarse2, 2))
     wait(send_sem, 2, tiles_of(geo_coarse3, 2))
+    wait(send_sem, 11, tiles_of(geo_middle3, 2))
+    wait(send_sem, 13, tiles_of(geo_outer3, 2))
     wait(send_sem, 3, tiles_of(geo_rhs2, 1))
     wait(send_sem, 4, tiles_of(geo_iter1, 1))
-    wait(send_sem, 5, tiles_of(geo_coarse3, 1))
+    wait(send_sem, 5, tiles_of(geo_rhs3, 1))
     wait(send_sem, 6, tiles_of(geo_coarse2, 1))
     wait_spread(send_sem, 7, bound_y, ny)
-    wait_spread(send_sem, 8, bound_x, nx)
+    wait_spread(send_sem, 8, few, 9)
+    wait_spread(send_sem, 12, more, 3)
+    wait_spread(send_sem, 14, last, 2)
     wait_spread(send_sem, 9, gram_y, ny)
     wait_spread(send_sem, 10, gram_x, nx)
 
@@ -522,9 +541,9 @@
                 vmem(3, 10, 64, 128), vmem(2, 10, 48, 128), vmem(2, 15, 40, 128), vmem(10, 48, 128), vmem(15, 40, 128),
                 *one, *two, *three,
                 vmem(8 * ROWS, 128), vmem(8 * ROWS, 128),
-                vmem(ny, 1, 128), vmem(nx, 1, 128), vmem(ny, 1, 128), vmem(nx, 1, 128),
+                vmem(ny, 1, 128), vmem(9, 1, 128), vmem(3, 1, 128), vmem(2, 1, 128), vmem(ny, 1, 128), vmem(nx, 1, 128),
                 vmem(2 * ROWS, 128), vmem(140, 8, 128),
-                pltpu.SemaphoreType.DMA((3,)), pltpu.SemaphoreType.DMA((11,)), pltpu.SemaphoreType.DMA((11,)),
+                pltpu.SemaphoreType.DMA((3,)), pltpu.SemaphoreType.DMA((15,)), pltpu.SemaphoreType.DMA((15,)),
             ],
             compiler_params=pltpu.CompilerParams(collective_id=0, has_side_effects=True, vmem_limit_bytes=40 * 2**20),
         )(*[pltpu.with_memory_space_constraint(x, pltpu.HBM) for x in (source, beta, shift)])

time: 57.5 us -> 57.7 us (level)
  no operation moved by 1% of the time
where the time goes in v3:
time: 57.7 us; the launch traced here: 57.5 us
  Pallas kernels  56.9 us (99%)
  local copies, waits for them, and re-layouts  0.63 us (1%)
    pallas_call x1, Pallas kernels, on_device(): pl.pallas_call(functools.partial(kernel, (nx, ny)), out_shape=jax.ShapeDt...  56.9 us

profile of v3, /device:TPU:1, one launch (start us, length us, event | category | flops | bytes accessed | tf_op | source)
XLA Modules:
  0.0 57.5 jit_solution(9077692429487356804)
XLA Ops:
  0.0 56.9 %shard_map.37 = f32[4,32,128]{2,1,0:T(8,128)S(1)} custom-call(f32[4,32,128]{2,1,0:T(8,128)} %source.1, f32[4,32,128]{2,1,0:T(8,128)} %beta.1, f32[4,32,128]{2,1,0:T(8,128)} %shift.1), custom_call_target="tpu_custom_call" | custom-call | tf_op jit(solution)/shard_map/pallas_call | solution.py:535
  56.9 0.6 %copy.5 = f32[4,32,128]{2,1,0:T(8,128)} copy(f32[4,32,128]{2,1,0:T(8,128)S(1)} %shard_map.37) | data formatting | bytes 131072

commit v4 on v3

--- a/solution.py
+++ b/solution.py
@@ -145,13 +145,14 @@
         else:
             start, planes = 0, min(count, reach + (dx + 1) * count)
             target = first - dx * count
-        row, high, to = (EDGE, rows, EDGE) if dy == 0 else (EDGE + rows - 8, 8, EDGE - 8) if dy > 0 else (EDGE, 8, EDGE + rows)
+        edge = 4 if count == 1 and abs(dx) > 3 else 8
+        row, high, to = (EDGE, rows, EDGE) if dy == 0 else (EDGE + rows - edge, edge, EDGE - edge) if dy > 0 else (EDGE, edge, EDGE + rows)
         out.append((dx, dy, first + start, target, planes, row, to, high))
     return out
 
 
 def tiles_of(geometry, fields):
-    return sum(fields * w[4] * w[7] // 8 for w in geometry)
+    return fields * sum(w[4] * w[7] for w in geometry) // 8
 
 
 def kernel(
@@ -160,7 +161,7 @@
     masked1, wx1, wy1, wz1, diag1, inv1, step1, near1, iter1, start1,
     masked2, wx2, wy2, wz2, diag2, inv2, step2, near2, iter2, start2, sum2,
     masked3, wx3, wy3, wz3, own3, inside3, basis, sol3,
-    pair_high, pair_low, bound_y, few, more, last, gram_y, gram_x, scalars, dummy,
+    pair_high, pair_low, bound_y, bound_x, gram_y, gram_x, scalars, dummy,
     load_sem, send_sem, recv_sem,
 ):
     nx, ny = counts
@@ -173,8 +174,6 @@
     over_y, over_x = ring(ny, 0), ring(nx, 1)
     middle = [o for o in far if 3 <= abs(o[0]) <= 4]
     outer = [o for o in far if abs(o[0]) > 4]
-    few_x = [(d, 0) for d in (4, -4, 3, -3, 2, -2, 1, -1)]
-    more_x, last_x = [(8, 0), (-8, 0)], [(nx // 2, 0)]
 
     loads = [
         pltpu.make_async_copy(ref, fields.at[n, pl.ds(3, 4), pl.ds(EDGE, 32)], load_sem.at[n])
@@ -183,7 +182,7 @@
     for load in loads:
         load.start()
 
-    partners = sorted({(dx, dy % ny) for dx, dy in wide + over_y}, key=lambda o: abs(o[0]) + min(o[1], ny - o[1]))
+    partners = sorted({(dx % nx, dy % ny) for dx, dy in far + over_y + over_x}, key=lambda o: min(o[0], nx - o[0]) + min(o[1], ny - o[1]))
     barrier = pltpu.get_barrier_semaphore()
     for dx, dy in partners:
         pl.semaphore_signal(barrier, 1, device_id=device(-dx, -dy), device_id_type=MESH)
@@ -202,10 +201,10 @@
         part = dummy.at[pl.ds(0, tiles)]
         pltpu.make_async_copy(part, part, sems.at[phase]).wait()
 
-    def spread(phase, ref, offsets, slots=None):
-        for n, (dx, dy) in enumerate(offsets):
+    def spread(phase, ref, offsets):
+        for dx, dy in offsets:
             pltpu.make_async_remote_copy(
-                src_ref=ref.at[0], dst_ref=ref.at[max(dx, dy) if slots is None else 1 + n], send_sem=send_sem.at[phase], recv_sem=recv_sem.at[phase],
+                src_ref=ref.at[0], dst_ref=ref.at[max(dx, dy)], send_sem=send_sem.at[phase], recv_sem=recv_sem.at[phase],
                 device_id=device(dx, dy), device_id_type=MESH,
             ).start()
 
@@ -293,10 +292,6 @@
     send(2, coarse3, geo_coarse3, True)
 
     wait(recv_sem, 0, tiles_of(geo_fields, 3))
-    wait(recv_sem, 1, tiles_of(geo_coarse2, 2))
-    wait_spread(recv_sem, 7, bound_y, ny)
-    few[0] = functools.reduce(jnp.maximum, [bound_y[n] for n in range(ny)])
-    spread(8, few, few_x, True)
     send(11, coarse3, geo_middle3, True)
     level1 = (masked1, wx1, wy1, wz1, diag1, inv1)
     prepare(
@@ -345,14 +340,15 @@
     loop(3, 7, keep1)
     send(4, iter1, geo_iter1, False)
 
+    send(13, coarse3, geo_outer3, True)
+    wait_spread(recv_sem, 7, bound_y, ny)
+    bound_x[0] = functools.reduce(jnp.maximum, [bound_y[n] for n in range(ny)])
+    spread(8, bound_x, over_x)
+    wait(recv_sem, 1, tiles_of(geo_coarse2, 2))
     level2 = (masked2, wx2, wy2, wz2, diag2, inv2)
     prepare(
         level2, (lambda p: coarse2[0, p, pl.ds(8, 32), :], lambda p: coarse2[1, p, pl.ds(8, 32), :]), 32, 4, (2, 16), PLANE_SCALES[1]
     )
-    wait_spread(recv_sem, 8, few, 9)
-    more[0] = functools.reduce(jnp.maximum, [few[n] for n in range(9)])
-    spread(12, more, more_x, True)
-    send(13, coarse3, geo_outer3, True)
     wait(recv_sem, 3, tiles_of(geo_rhs2, 1))
     loop(2, 8, first_step(step2, inv2, lambda p: rhs2_at(p, 8, 32), 32))
 
@@ -368,14 +364,11 @@
         iter2[p, pl.ds(EDGE, 16), :] = near2[p, pl.ds(EDGE, 16), :]
     send(6, iter2, geo_coarse2, False)
 
-    wait_spread(recv_sem, 12, more, 3)
-    last[0] = functools.reduce(jnp.maximum, [more[n] for n in range(3)])
-    spread(14, last, last_x, True)
     wait(recv_sem, 2, tiles_of(geo_coarse3, 2))
     wait(recv_sem, 11, tiles_of(geo_middle3, 2))
     wait(recv_sem, 13, tiles_of(geo_outer3, 2))
-    wait_spread(recv_sem, 14, last, 2)
-    scale = 2.0 / jnp.maximum(last[0], last[1])
+    wait_spread(recv_sem, 8, bound_x, nx)
+    scale = 2.0 / functools.reduce(jnp.maximum, [bound_x[n] for n in range(nx)])
 
     def clean3(p):
         ok = inside(p, 24, 8, 7, 15, 1, 8)
@@ -514,9 +507,7 @@
     wait(send_sem, 5, tiles_of(geo_rhs3, 1))
     wait(send_sem, 6, tiles_of(geo_coarse2, 1))
     wait_spread(send_sem, 7, bound_y, ny)
-    wait_spread(send_sem, 8, few, 9)
-    wait_spread(send_sem, 12, more, 3)
-    wait_spread(send_sem, 14, last, 2)
+    wait_spread(send_sem, 8, bound_x, nx)
     wait_spread(send_sem, 9, gram_y, ny)
     wait_spread(send_sem, 10, gram_x, nx)
 
@@ -541,7 +532,7 @@
                 vmem(3, 10, 64, 128), vmem(2, 10, 48, 128), vmem(2, 15, 40, 128), vmem(10, 48, 128), vmem(15, 40, 128),
                 *one, *two, *three,
                 vmem(8 * ROWS, 128), vmem(8 * ROWS, 128),
-                vmem(ny, 1, 128), vmem(9, 1, 128), vmem(3, 1, 128), vmem(2, 1, 128), vmem(ny, 1, 128), vmem(nx, 1, 128),
+                vmem(ny, 1, 128), vmem(nx, 1, 128), vmem(ny, 1, 128), vmem(nx, 1, 128),
                 vmem(2 * ROWS, 128), vmem(140, 8, 128),
                 pltpu.SemaphoreType.DMA((3,)), pltpu.SemaphoreType.DMA((15,)), pltpu.SemaphoreType.DMA((15,)),
             ],

time: 57.7 us -> 53.8 us (0.932)
  Pallas kernels: 56.9 us -> 53 us
    pallas_call x1, Pallas kernels: 56.9 us -> 53 us  [on_device(): pl.pallas_call(functools.partial(kernel, (nx, ny)), out_shape=jax.ShapeDt...]
where the time goes in v4:
time: 53.8 us; the launch traced here: 53.7 us
  Pallas kernels  53 us (99%)
  local copies, waits for them, and re-layouts  0.63 us (1%)
    pallas_call x1, Pallas kernels, on_device(): pl.pallas_call(functools.partial(kernel, (nx, ny)), out_shape=jax.ShapeDt...  53 us

profile of v4, /device:TPU:1, one launch (start us, length us, event | category | flops | bytes accessed | tf_op | source)
XLA Modules:
  0.0 53.7 jit_solution(16083411750229155607)
XLA Ops:
  0.0 53.0 %shard_map.37 = f32[4,32,128]{2,1,0:T(8,128)S(1)} custom-call(f32[4,32,128]{2,1,0:T(8,128)} %source.1, f32[4,32,128]{2,1,0:T(8,128)} %beta.1, f32[4,32,128]{2,1,0:T(8,128)} %shift.1), custom_call_target="tpu_custom_call" | custom-call | tf_op jit(solution)/shard_map/pallas_call | solution.py:526
  53.0 0.6 %copy.5 = f32[4,32,128]{2,1,0:T(8,128)} copy(f32[4,32,128]{2,1,0:T(8,128)S(1)} %shard_map.37) | data formatting | bytes 131072

commit v5 on v4

--- a/solution.py
+++ b/solution.py
@@ -161,7 +161,7 @@
     masked1, wx1, wy1, wz1, diag1, inv1, step1, near1, iter1, start1,
     masked2, wx2, wy2, wz2, diag2, inv2, step2, near2, iter2, start2, sum2,
     masked3, wx3, wy3, wz3, own3, inside3, basis, sol3,
-    pair_high, pair_low, bound_y, bound_x, gram_y, gram_x, scalars, dummy,
+    pair_high, pair_low, bound_y, few, more, gram_y, gram_x, scalars, dummy,
     load_sem, send_sem, recv_sem,
 ):
     nx, ny = counts
@@ -171,7 +171,11 @@
         return lax.rem(gx + (dx + nx), nx), lax.rem(gy + (dy + ny), ny)
 
     near, wide, far = box(1, 1), box(2, 1), box(7, 1)
-    over_y, over_x = ring(ny, 0), ring(nx, 1)
+    over_y = ring(ny, 0)
+    over_z = [(2 * n, 0) for n, _ in ring(nx // 2, 1)]
+    along_x = [(d, 0) for d in range(-8, 9) if d]
+    few_x = [(d, 0) for n in range(6, 0, -1) for d in (n, -n)]
+    more_x = [(13, 0), (-13, 0)]
     middle = [o for o in far if 3 <= abs(o[0]) <= 4]
     outer = [o for o in far if abs(o[0]) > 4]
 
@@ -182,7 +186,7 @@
     for load in loads:
         load.start()
 
-    partners = sorted({(dx % nx, dy % ny) for dx, dy in far + over_y + over_x}, key=lambda o: min(o[0], nx - o[0]) + min(o[1], ny - o[1]))
+    partners = sorted({(dx % nx, dy % ny) for dx, dy in wide + over_y + along_x}, key=lambda o: min(o[0], nx - o[0]) + min(o[1], ny - o[1]))
     barrier = pltpu.get_barrier_semaphore()
     for dx, dy in partners:
         pl.semaphore_signal(barrier, 1, device_id=device(-dx, -dy), device_id_type=MESH)
@@ -201,10 +205,10 @@
         part = dummy.at[pl.ds(0, tiles)]
         pltpu.make_async_copy(part, part, sems.at[phase]).wait()
 
-    def spread(phase, ref, offsets):
-        for dx, dy in offsets:
+    def spread(phase, ref, offsets, slots=None):
+        for n, (dx, dy) in enumerate(offsets):
             pltpu.make_async_remote_copy(
-                src_ref=ref.at[0], dst_ref=ref.at[max(dx, dy)], send_sem=send_sem.at[phase], recv_sem=recv_sem.at[phase],
+                src_ref=ref.at[0], dst_ref=ref.at[max(dx, dy) if slots is None else slots[n]], send_sem=send_sem.at[phase], recv_sem=recv_sem.at[phase],
                 device_id=device(dx, dy), device_id_type=MESH,
             ).start()
 
@@ -292,6 +296,9 @@
     send(2, coarse3, geo_coarse3, True)
 
     wait(recv_sem, 0, tiles_of(geo_fields, 3))
+    wait_spread(recv_sem, 7, bound_y, ny)
+    few[0] = functools.reduce(jnp.maximum, [bound_y[n] for n in range(ny)])
+    spread(8, few, few_x, range(1, 13))
     send(11, coarse3, geo_middle3, True)
     level1 = (masked1, wx1, wy1, wz1, diag1, inv1)
     prepare(
@@ -341,9 +348,6 @@
     send(4, iter1, geo_iter1, False)
 
     send(13, coarse3, geo_outer3, True)
-    wait_spread(recv_sem, 7, bound_y, ny)
-    bound_x[0] = functools.reduce(jnp.maximum, [bound_y[n] for n in range(ny)])
-    spread(8, bound_x, over_x)
     wait(recv_sem, 1, tiles_of(geo_coarse2, 2))
     level2 = (masked2, wx2, wy2, wz2, diag2, inv2)
     prepare(
@@ -364,11 +368,14 @@
         iter2[p, pl.ds(EDGE, 16), :] = near2[p, pl.ds(EDGE, 16), :]
     send(6, iter2, geo_coarse2, False)
 
+    wait_spread(recv_sem, 8, few, 13)
+    more[0] = functools.reduce(jnp.maximum, [few[n] for n in range(13)])
+    spread(12, more, more_x, range(1, 3))
     wait(recv_sem, 2, tiles_of(geo_coarse3, 2))
     wait(recv_sem, 11, tiles_of(geo_middle3, 2))
     wait(recv_sem, 13, tiles_of(geo_outer3, 2))
-    wait_spread(recv_sem, 8, bound_x, nx)
-    scale = 2.0 / functools.reduce(jnp.maximum, [bound_x[n] for n in range(nx)])
+    wait_spread(recv_sem, 12, more, 3)
+    scale = 2.0 / functools.reduce(jnp.maximum, [more[n] for n in range(3)])
 
     def clean3(p):
         ok = inside(p, 24, 8, 7, 15, 1, 8)
@@ -441,14 +448,20 @@
         s, t = tree([(ref[n], zero) for n in range(count)])
         return s + jnp.where(lane_of((1, 128)) >= 64, pltpu.roll(t, 64, 1), 0.0)
 
-    spread(9, gram_y, over_y)
-    wait_spread(recv_sem, 9, gram_y, ny)
-    gram_x[0] = total_of(gram_y, ny)
-    spread(10, gram_x, over_x)
+    sibling = gx + 1 - 2 * lax.rem(gx, 2)
+    for column, y in [(n, dy) for _, dy in over_y + [(0, 0)] for n in (1, 0)]:
+        if column or y:
+            pltpu.make_async_remote_copy(
+                src_ref=gram_y.at[0], dst_ref=gram_y.at[column * ny + y], send_sem=send_sem.at[9], recv_sem=recv_sem.at[9],
+                device_id=(sibling if column else gx, device(0, y)[1]), device_id_type=MESH,
+            ).start()
+    wait_spread(recv_sem, 9, gram_y, 2 * ny)
+    gram_x[0] = total_of(gram_y, 2 * ny)
+    spread(10, gram_x, over_z, [n // 2 for n, _ in over_z])
     wait(recv_sem, 4, tiles_of(geo_iter1, 1))
     wait(recv_sem, 6, tiles_of(geo_coarse2, 1))
-    wait_spread(recv_sem, 10, gram_x, nx)
-    entries = jnp.broadcast_to(total_of(gram_x, nx), (2 * ROWS, 128))
+    wait_spread(recv_sem, 10, gram_x, nx // 2)
+    entries = jnp.broadcast_to(total_of(gram_x, nx // 2), (2 * ROWS, 128))
     lane, row = lane_of((2 * ROWS, 128)), lax.broadcasted_iota(jnp.int32, (2 * ROWS, 128), 0)
     place = jnp.where(row < ROWS, row, row + (64 - ROWS))
     column = jnp.sum(jnp.where(lane == place, entries, 0.0), axis=1, keepdims=True)
@@ -507,9 +520,10 @@
     wait(send_sem, 5, tiles_of(geo_rhs3, 1))
     wait(send_sem, 6, tiles_of(geo_coarse2, 1))
     wait_spread(send_sem, 7, bound_y, ny)
-    wait_spread(send_sem, 8, bound_x, nx)
-    wait_spread(send_sem, 9, gram_y, ny)
-    wait_spread(send_sem, 10, gram_x, nx)
+    wait_spread(send_sem, 8, few, 13)
+    wait_spread(send_sem, 12, more, 3)
+    wait_spread(send_sem, 9, gram_y, 2 * ny)
+    wait_spread(send_sem, 10, gram_x, nx // 2)
 
 
 def solution(mesh):
@@ -532,7 +546,7 @@
                 vmem(3, 10, 64, 128), vmem(2, 10, 48, 128), vmem(2, 15, 40, 128), vmem(10, 48, 128), vmem(15, 40, 128),
                 *one, *two, *three,
                 vmem(8 * ROWS, 128), vmem(8 * ROWS, 128),
-                vmem(ny, 1, 128), vmem(nx, 1, 128), vmem(ny, 1, 128), vmem(nx, 1, 128),
+                vmem(ny, 1, 128), vmem(13, 1, 128), vmem(3, 1, 128), vmem(2 * ny, 1, 128), vmem(nx // 2, 1, 128),
                 vmem(2 * ROWS, 128), vmem(140, 8, 128),
                 pltpu.SemaphoreType.DMA((3,)), pltpu.SemaphoreType.DMA((15,)), pltpu.SemaphoreType.DMA((15,)),
             ],

time: 53.8 us -> 51.9 us (0.965)
  Pallas kernels: 53 us -> 51.1 us
    pallas_call x1, Pallas kernels: 53 us -> 51.1 us  [on_device(): pl.pallas_call(functools.partial(kernel, (nx, ny)), out_shape=jax.ShapeDt...]
where the time goes in v5:
time: 51.9 us; the launch traced here: 51.7 us
  Pallas kernels  51.1 us (98%)
  local copies, waits for them, and re-layouts  0.63 us (1%)
    pallas_call x1, Pallas kernels, on_device(): pl.pallas_call(functools.partial(kernel, (nx, ny)), out_shape=jax.ShapeDt...  51.1 us

profile of v5, /device:TPU:1, one launch (start us, length us, event | category | flops | bytes accessed | tf_op | source)
XLA Modules:
  0.0 51.7 jit_solution(15057941885112881107)
XLA Ops:
  0.0 51.1 %shard_map.37 = f32[4,32,128]{2,1,0:T(8,128)S(1)} custom-call(f32[4,32,128]{2,1,0:T(8,128)} %source.1, f32[4,32,128]{2,1,0:T(8,128)} %beta.1, f32[4,32,128]{2,1,0:T(8,128)} %shift.1), custom_call_target="tpu_custom_call" | custom-call | tf_op jit(solution)/shard_map/pallas_call | solution.py:540
  51.1 0.6 %copy.5 = f32[4,32,128]{2,1,0:T(8,128)} copy(f32[4,32,128]{2,1,0:T(8,128)S(1)} %shard_map.37) | data formatting | bytes 131072

commit v6 on v5

--- a/solution.py
+++ b/solution.py
@@ -17,6 +17,7 @@
 PLANE_SCALES = (1.0, 0.25, 0.0625)
 EDGE = 16
 SPLIT = 4097.0
+SOON = 2
 
 PAIRS = [(i, j) for i in range(ITERS) for j in range(i, ITERS)] + [(ITERS - 1, ITERS)]
 SLOT = {pair: n for n, pair in enumerate(PAIRS)}
@@ -160,7 +161,7 @@
     fields, coarse2, coarse3, rhs2, rhs3,
     masked1, wx1, wy1, wz1, diag1, inv1, step1, near1, iter1, start1,
     masked2, wx2, wy2, wz2, diag2, inv2, step2, near2, iter2, start2, sum2,
-    masked3, wx3, wy3, wz3, own3, inside3, basis, sol3,
+    masked3, wx3, wy3, wz3, own3, inside3, basis, lifted,
     pair_high, pair_low, bound_y, few, more, gram_y, gram_x, scalars, dummy,
     load_sem, send_sem, recv_sem,
 ):
@@ -252,14 +253,14 @@
             masked[p, pl.ds(8, rows), :] = jnp.where(ok, beta_at(p), 0.0)
 
         def fill(p):
-            wxp, wyp, wzp, total = weights(masked, p, 8, rows, 0.5 * scale, 0.5 * VERTICAL)
+            wxp, wyp, wzp, total = weights(masked, p, 12, rows - 8, 0.5 * scale, 0.5 * VERTICAL)
             total = total + shift_at(p)
-            wx[p, pl.ds(8, rows), :] = wxp
-            wy[p, pl.ds(8, rows), :] = wyp
-            wz[p, pl.ds(8, rows), :] = wzp
-            diag[p, pl.ds(8, rows), :] = total
-            ok = inside(p, rows, 8, first, 10, own[0], own[1])
-            inv[p, pl.ds(8, rows), :] = jnp.where(ok, 1.0 / total, 0.0)
+            wx[p, pl.ds(12, rows - 8), :] = wxp
+            wy[p, pl.ds(12, rows - 8), :] = wyp
+            wz[p, pl.ds(12, rows - 8), :] = wzp
+            diag[p, pl.ds(12, rows - 8), :] = total
+            ok = inside(p, rows - 8, 12, first, 10, own[0], own[1])
+            inv[p, pl.ds(12, rows - 8), :] = jnp.where(ok, 1.0 / total, 0.0)
 
         loop(0, 10, clean)
         loop(1, 9, fill)
@@ -296,68 +297,68 @@
     send(2, coarse3, geo_coarse3, True)
 
     wait(recv_sem, 0, tiles_of(geo_fields, 3))
+    level1 = (masked1, wx1, wy1, wz1, diag1, inv1)
+    prepare(
+        level1, (lambda p: fields[1, p, pl.ds(12, 40), :], lambda p: fields[2, p, pl.ds(8, 48), :]), 48, 3, (4, 32), PLANE_SCALES[0]
+    )
+
+    def first_step(step, inv, value, rows):
+        def body(p):
+            step[p, pl.ds(12, rows), :] = FIRST * value(p) * inv[p, pl.ds(12, rows), :]
+
+        return body
+
+    def smooth(step, wx, wy, wz, inv, p, low, rows):
+        part = off(step, wx, wy, wz, p, low, rows)
+        return KEEP * step[p, pl.ds(low, rows), :] + SECOND * inv[p, pl.ds(low, rows), :] * part
+
+    loop(1, 9, first_step(step1, inv1, lambda p: fields[0, p, pl.ds(12, 40), :], 40))
+
+    def presmooth1(p):
+        near1[p, pl.ds(12, 40), :] = smooth(step1, wx1, wy1, wz1, inv1, p, 12, 40)
+
+    loop(2, 8, presmooth1)
+
+    def residual(f, v, level, p, low, rows):
+        _, wx, wy, wz, diag, _ = level
+        value = f(p, low, rows) - diag[p, pl.ds(low, rows), :] * v[p, pl.ds(low, rows), :]
+        return value + off(v, wx, wy, wz, p, low, rows)
+
+    def source_at(p, low, rows):
+        return fields[0, p, pl.ds(low, rows), :]
+
+    def rhs2_at(p, low, rows):
+        return rhs2[p, pl.ds(low, rows), :]
+
+    def restrict1(q):
+        both = residual(source_at, near1, level1, 3 + 2 * q, EDGE, 32) + residual(source_at, near1, level1, 4 + 2 * q, EDGE, 32)
+        start1[q, pl.ds(EDGE, 32), :] = both
+        rhs2[4 + q, pl.ds(EDGE, 16), :] = coarsen_rows(start1, q, 32)
+
+    loop(0, 2, restrict1)
+    send(3, rhs2, geo_rhs2, False)
+
+    def keep1(p):
+        iter1[p, pl.ds(EDGE, 32), :] = near1[p, pl.ds(EDGE, 32), :]
+
+    loop(3, 7, keep1)
+    send(4, iter1, geo_iter1, False)
+
     wait_spread(recv_sem, 7, bound_y, ny)
     few[0] = functools.reduce(jnp.maximum, [bound_y[n] for n in range(ny)])
     spread(8, few, few_x, range(1, 13))
     send(11, coarse3, geo_middle3, True)
-    level1 = (masked1, wx1, wy1, wz1, diag1, inv1)
-    prepare(
-        level1, (lambda p: fields[1, p, pl.ds(8, 48), :], lambda p: fields[2, p, pl.ds(8, 48), :]), 48, 3, (4, 32), PLANE_SCALES[0]
-    )
-
-    def first_step(step, inv, value, rows):
-        def body(p):
-            step[p, pl.ds(8, rows), :] = FIRST * value(p) * inv[p, pl.ds(8, rows), :]
-
-        return body
-
-    def smooth(step, wx, wy, wz, inv, p, low, rows):
-        part = off(step, wx, wy, wz, p, low, rows)
-        return KEEP * step[p, pl.ds(low, rows), :] + SECOND * inv[p, pl.ds(low, rows), :] * part
-
-    loop(1, 9, first_step(step1, inv1, lambda p: fields[0, p, pl.ds(8, 48), :], 48))
-
-    def presmooth1(p):
-        near1[p, pl.ds(8, 48), :] = smooth(step1, wx1, wy1, wz1, inv1, p, 8, 48)
-
-    loop(2, 8, presmooth1)
-
-    def residual(f, v, level, p, low, rows):
-        _, wx, wy, wz, diag, _ = level
-        value = f(p, low, rows) - diag[p, pl.ds(low, rows), :] * v[p, pl.ds(low, rows), :]
-        return value + off(v, wx, wy, wz, p, low, rows)
-
-    def source_at(p, low, rows):
-        return fields[0, p, pl.ds(low, rows), :]
-
-    def rhs2_at(p, low, rows):
-        return rhs2[p, pl.ds(low, rows), :]
-
-    def restrict1(q):
-        both = residual(source_at, near1, level1, 3 + 2 * q, EDGE, 32) + residual(source_at, near1, level1, 4 + 2 * q, EDGE, 32)
-        start1[q, pl.ds(EDGE, 32), :] = both
-        rhs2[4 + q, pl.ds(EDGE, 16), :] = coarsen_rows(start1, q, 32)
-
-    loop(0, 2, restrict1)
-    send(3, rhs2, geo_rhs2, False)
-
-    def keep1(p):
-        iter1[p, pl.ds(EDGE, 32), :] = near1[p, pl.ds(EDGE, 32), :]
-
-    loop(3, 7, keep1)
-    send(4, iter1, geo_iter1, False)
-
     send(13, coarse3, geo_outer3, True)
     wait(recv_sem, 1, tiles_of(geo_coarse2, 2))
     level2 = (masked2, wx2, wy2, wz2, diag2, inv2)
     prepare(
-        level2, (lambda p: coarse2[0, p, pl.ds(8, 32), :], lambda p: coarse2[1, p, pl.ds(8, 32), :]), 32, 4, (2, 16), PLANE_SCALES[1]
+        level2, (lambda p: coarse2[0, p, pl.ds(12, 24), :], lambda p: coarse2[1, p, pl.ds(8, 32), :]), 32, 4, (2, 16), PLANE_SCALES[1]
     )
     wait(recv_sem, 3, tiles_of(geo_rhs2, 1))
-    loop(2, 8, first_step(step2, inv2, lambda p: rhs2_at(p, 8, 32), 32))
+    loop(2, 8, first_step(step2, inv2, lambda p: rhs2_at(p, 12, 24), 24))
 
     def presmooth2(p):
-        near2[p, pl.ds(8, 32), :] = smooth(step2, wx2, wy2, wz2, inv2, p, 8, 32)
+        near2[p, pl.ds(12, 24), :] = smooth(step2, wx2, wy2, wz2, inv2, p, 12, 24)
 
     loop(3, 7, presmooth2)
     both = residual(rhs2_at, near2, level2, 4, EDGE, 16) + residual(rhs2_at, near2, level2, 5, EDGE, 16)
@@ -455,11 +456,64 @@
                 src_ref=gram_y.at[0], dst_ref=gram_y.at[column * ny + y], send_sem=send_sem.at[9], recv_sem=recv_sem.at[9],
                 device_id=(sibling if column else gx, device(0, y)[1]), device_id_type=MESH,
             ).start()
+    def lift(k):
+        start = isinstance(k, int)
+
+        def prolong2(p):
+            if start:
+                value = iter2[p, pl.ds(12, 24), :]
+            else:
+                coarse = basis[k, 5 + p // 2, pl.ds(14, 12), :]
+                start2[p, pl.ds(12, 12, stride=2), :] = coarse
+                start2[p, pl.ds(13, 12, stride=2), :] = coarse
+                value = start2[p, pl.ds(12, 24), :]
+            start2[p, pl.ds(12, 24), :] = jnp.where(inside(p, 24, 12, 4, 10, 2, 16), value, 0.0)
+
+        def zero(p, low, rows):
+            return jnp.zeros((rows, 128), jnp.float32)
+
+        loop(1, 9, prolong2)
+        rhs = rhs2_at if start else zero
+        loop(2, 8, first_step(step2, inv2, lambda p: residual(rhs, start2, level2, p, 12, 24), 24))
+
+        def post2(p):
+            sum2[p, pl.ds(12, 24), :] = start2[p, pl.ds(12, 24), :] + smooth(step2, wx2, wy2, wz2, inv2, p, 12, 24)
+
+        loop(3, 7, post2)
+
+        def prolong1(p):
+            coarse = sum2[(p + 5) // 2, pl.ds(14, 20), :]
+            start1[p, pl.ds(12, 20, stride=2), :] = coarse
+            start1[p, pl.ds(13, 20, stride=2), :] = coarse
+            value = start1[p, pl.ds(12, 40), :]
+            if start:
+                value = value + iter1[p, pl.ds(12, 40), :]
+            start1[p, pl.ds(12, 40), :] = jnp.where(inside(p, 40, 12, 3, 10, 4, 32), value, 0.0)
+
+        loop(1, 9, prolong1)
+        side = source_at if start else zero
+        loop(2, 8, first_step(step1, inv1, lambda p: residual(side, start1, level1, p, 12, 40), 40))
+
+        def post1(p):
+            lifted[k, p - 3] = start1[p, pl.ds(EDGE, 32), :] + smooth(step1, wx1, wy1, wz1, inv1, p, EDGE, 32)
+
+        loop(3, 7, post1)
+
+    def lift_some(low, high):
+        def step(k, carry):
+            lift(k)
+            return carry
+
+        lax.fori_loop(low, high, step, 0)
+
+    wait(recv_sem, 4, tiles_of(geo_iter1, 1))
+    wait(recv_sem, 6, tiles_of(geo_coarse2, 1))
+    lift(ITERS)
+    lift_some(0, SOON)
     wait_spread(recv_sem, 9, gram_y, 2 * ny)
     gram_x[0] = total_of(gram_y, 2 * ny)
     spread(10, gram_x, over_z, [n // 2 for n, _ in over_z])
-    wait(recv_sem, 4, tiles_of(geo_iter1, 1))
-    wait(recv_sem, 6, tiles_of(geo_coarse2, 1))
+    lift_some(SOON, ITERS)
     wait_spread(recv_sem, 10, gram_x, nx // 2)
     entries = jnp.broadcast_to(total_of(gram_x, nx // 2), (2 * ROWS, 128))
     lane, row = lane_of((2 * ROWS, 128)), lax.broadcasted_iota(jnp.int32, (2 * ROWS, 128), 0)
@@ -473,42 +527,11 @@
 
     answer = [value * scale for value in gradient_coefficients(gram)]
 
-    for n in range(5):
-        p = 5 + n
-        total = answer[0] * basis[0, p, pl.ds(8, 24), :]
-        for k in range(1, ITERS):
-            total = total + answer[k] * basis[k, p, pl.ds(8, 24), :]
-        sol3[n, pl.ds(8, 24), :] = total
-
-    def prolong2(p):
-        value = sol3[p // 2, pl.ds(12, 16), :]
-        start2[p, pl.ds(8, 16, stride=2), :] = value
-        start2[p, pl.ds(9, 16, stride=2), :] = value
-        ok = inside(p, 32, 8, 4, 10, 2, 16)
-        start2[p, pl.ds(8, 32), :] = jnp.where(ok, start2[p, pl.ds(8, 32), :] + iter2[p, pl.ds(8, 32), :], 0.0)
-
-    loop(1, 9, prolong2)
-    loop(2, 8, first_step(step2, inv2, lambda p: residual(rhs2_at, start2, level2, p, 8, 32), 32))
-
-    def post2(p):
-        sum2[p, pl.ds(8, 32), :] = start2[p, pl.ds(8, 32), :] + smooth(step2, wx2, wy2, wz2, inv2, p, 8, 32)
-
-    loop(3, 7, post2)
-
-    def prolong1(p):
-        value = sum2[(p + 5) // 2, pl.ds(12, 24), :]
-        start1[p, pl.ds(8, 24, stride=2), :] = value
-        start1[p, pl.ds(9, 24, stride=2), :] = value
-        ok = inside(p, 48, 8, 3, 10, 4, 32)
-        start1[p, pl.ds(8, 48), :] = jnp.where(ok, start1[p, pl.ds(8, 48), :] + iter1[p, pl.ds(8, 48), :], 0.0)
-
-    loop(1, 9, prolong1)
-    loop(2, 8, first_step(step1, inv1, lambda p: residual(source_at, start1, level1, p, 8, 48), 48))
-
-    def post1(p):
-        out[p - 3] = start1[p, pl.ds(EDGE, 32), :] + smooth(step1, wx1, wy1, wz1, inv1, p, EDGE, 32)
-
-    loop(3, 7, post1)
+    for p in range(4):
+        total = lifted[ITERS, p]
+        for k in range(ITERS):
+            total = total + answer[k] * lifted[k, p]
+        out[p] = total
 
     wait(send_sem, 0, tiles_of(geo_fields, 3))
     wait(send_sem, 1, tiles_of(geo_coarse2, 2))
@@ -534,7 +557,7 @@
 
     one = [vmem(10, 64, 128)] * 10
     two = [vmem(10, 48, 128)] * 11
-    three = [vmem(15, 40, 128)] * 6 + [vmem(ITERS + 1, 15, 40, 128), vmem(5, 40, 128)]
+    three = [vmem(15, 40, 128)] * 6 + [vmem(ITERS + 1, 15, 40, 128), vmem(ITERS + 1, 4, 32, 128)]
 
     def on_device(source, beta, shift):
         return pl.pallas_call(

time: 51.9 us -> 50.8 us (0.979)
  Pallas kernels: 51.1 us -> 50 us
    pallas_call x1, Pallas kernels: 51.1 us -> 50 us  [on_device(): pl.pallas_call(functools.partial(kernel, (nx, ny)), out_shape=jax.ShapeDt...]
where the time goes in v6:
time: 50.8 us; the launch traced here: 50.6 us
  Pallas kernels  50 us (98%)
  local copies, waits for them, and re-layouts  0.63 us (1%)
    pallas_call x1, Pallas kernels, on_device(): pl.pallas_call(functools.partial(kernel, (nx, ny)), out_shape=jax.ShapeDt...  50 us

profile of v6, /device:TPU:1, one launch (start us, length us, event | category | flops | bytes accessed | tf_op | source)
XLA Modules:
  0.0 50.6 jit_solution(13587221224283447399)
XLA Ops:
  0.0 50.0 %shard_map.37 = f32[4,32,128]{2,1,0:T(8,128)S(1)} custom-call(f32[4,32,128]{2,1,0:T(8,128)} %source.1, f32[4,32,128]{2,1,0:T(8,128)} %beta.1, f32[4,32,128]{2,1,0:T(8,128)} %shift.1), custom_call_target="tpu_custom_call" | custom-call | tf_op jit(solution)/shard_map/pallas_call | solution.py:563
  50.0 0.6 %copy.5 = f32[4,32,128]{2,1,0:T(8,128)} copy(f32[4,32,128]{2,1,0:T(8,128)S(1)} %shard_map.37) | data formatting | bytes 131072

commit v7 on v6

--- a/solution.py
+++ b/solution.py
@@ -162,7 +162,7 @@
     masked1, wx1, wy1, wz1, diag1, inv1, step1, near1, iter1, start1,
     masked2, wx2, wy2, wz2, diag2, inv2, step2, near2, iter2, start2, sum2,
     masked3, wx3, wy3, wz3, own3, inside3, basis, lifted,
-    pair_high, pair_low, bound_y, few, more, gram_y, gram_x, scalars, dummy,
+    pair_high, pair_low, bound_y, few, more, last, gram_y, gram_x, scalars, dummy,
     load_sem, send_sem, recv_sem,
 ):
     nx, ny = counts
@@ -174,9 +174,8 @@
     near, wide, far = box(1, 1), box(2, 1), box(7, 1)
     over_y = ring(ny, 0)
     over_z = [(2 * n, 0) for n, _ in ring(nx // 2, 1)]
-    along_x = [(d, 0) for d in range(-8, 9) if d]
-    few_x = [(d, 0) for n in range(6, 0, -1) for d in (n, -n)]
-    more_x = [(13, 0), (-13, 0)]
+    few_x = [(d, 0) for n in range(4, 0, -1) for d in (n, -n)]
+    more_x, last_x = [(8, 0), (-8, 0)], [(nx // 2, 0)]
     middle = [o for o in far if 3 <= abs(o[0]) <= 4]
     outer = [o for o in far if abs(o[0]) > 4]
 
@@ -184,13 +183,14 @@
         pltpu.make_async_copy(ref, fields.at[n, pl.ds(3, 4), pl.ds(EDGE, 32)], load_sem.at[n])
         for n, ref in enumerate((source, shift, beta))
     ]
-    for load in loads:
-        load.start()
-
-    partners = sorted({(dx % nx, dy % ny) for dx, dy in wide + over_y + along_x}, key=lambda o: min(o[0], nx - o[0]) + min(o[1], ny - o[1]))
+
+    partners = sorted({(dx % nx, dy % ny) for dx, dy in wide + over_y}, key=lambda o: min(o[0], nx - o[0]) + min(o[1], ny - o[1]))
     barrier = pltpu.get_barrier_semaphore()
     for dx, dy in partners:
         pl.semaphore_signal(barrier, 1, device_id=device(-dx, -dy), device_id_type=MESH)
+
+    for load in loads:
+        load.start()
 
     def send(phase, ref, geometry, stacked):
         for dx, dy, plane, target, planes, row, to, high in geometry:
@@ -297,6 +297,10 @@
     send(2, coarse3, geo_coarse3, True)
 
     wait(recv_sem, 0, tiles_of(geo_fields, 3))
+    wait(recv_sem, 1, tiles_of(geo_coarse2, 2))
+    wait_spread(recv_sem, 7, bound_y, ny)
+    few[0] = functools.reduce(jnp.maximum, [bound_y[n] for n in range(ny)])
+    spread(8, few, few_x, range(1, 9))
     level1 = (masked1, wx1, wy1, wz1, diag1, inv1)
     prepare(
         level1, (lambda p: fields[1, p, pl.ds(12, 40), :], lambda p: fields[2, p, pl.ds(8, 48), :]), 48, 3, (4, 32), PLANE_SCALES[0]
@@ -344,16 +348,15 @@
     loop(3, 7, keep1)
     send(4, iter1, geo_iter1, False)
 
-    wait_spread(recv_sem, 7, bound_y, ny)
-    few[0] = functools.reduce(jnp.maximum, [bound_y[n] for n in range(ny)])
-    spread(8, few, few_x, range(1, 13))
     send(11, coarse3, geo_middle3, True)
-    send(13, coarse3, geo_outer3, True)
-    wait(recv_sem, 1, tiles_of(geo_coarse2, 2))
     level2 = (masked2, wx2, wy2, wz2, diag2, inv2)
     prepare(
         level2, (lambda p: coarse2[0, p, pl.ds(12, 24), :], lambda p: coarse2[1, p, pl.ds(8, 32), :]), 32, 4, (2, 16), PLANE_SCALES[1]
     )
+    wait_spread(recv_sem, 8, few, 9)
+    more[0] = functools.reduce(jnp.maximum, [few[n] for n in range(9)])
+    spread(12, more, more_x, range(1, 3))
+    send(13, coarse3, geo_outer3, True)
     wait(recv_sem, 3, tiles_of(geo_rhs2, 1))
     loop(2, 8, first_step(step2, inv2, lambda p: rhs2_at(p, 12, 24), 24))
 
@@ -369,14 +372,14 @@
         iter2[p, pl.ds(EDGE, 16), :] = near2[p, pl.ds(EDGE, 16), :]
     send(6, iter2, geo_coarse2, False)
 
-    wait_spread(recv_sem, 8, few, 13)
-    more[0] = functools.reduce(jnp.maximum, [few[n] for n in range(13)])
-    spread(12, more, more_x, range(1, 3))
+    wait_spread(recv_sem, 12, more, 3)
+    last[0] = functools.reduce(jnp.maximum, [more[n] for n in range(3)])
+    spread(14, last, last_x, range(1, 2))
     wait(recv_sem, 2, tiles_of(geo_coarse3, 2))
     wait(recv_sem, 11, tiles_of(geo_middle3, 2))
     wait(recv_sem, 13, tiles_of(geo_outer3, 2))
-    wait_spread(recv_sem, 12, more, 3)
-    scale = 2.0 / functools.reduce(jnp.maximum, [more[n] for n in range(3)])
+    wait_spread(recv_sem, 14, last, 2)
+    scale = 2.0 / jnp.maximum(last[0], last[1])
 
     def clean3(p):
         ok = inside(p, 24, 8, 7, 15, 1, 8)
@@ -543,8 +546,9 @@
     wait(send_sem, 5, tiles_of(geo_rhs3, 1))
     wait(send_sem, 6, tiles_of(geo_coarse2, 1))
     wait_spread(send_sem, 7, bound_y, ny)
-    wait_spread(send_sem, 8, few, 13)
+    wait_spread(send_sem, 8, few, 9)
     wait_spread(send_sem, 12, more, 3)
+    wait_spread(send_sem, 14, last, 2)
     wait_spread(send_sem, 9, gram_y, 2 * ny)
     wait_spread(send_sem, 10, gram_x, nx // 2)
 
@@ -569,7 +573,7 @@
                 vmem(3, 10, 64, 128), vmem(2, 10, 48, 128), vmem(2, 15, 40, 128), vmem(10, 48, 128), vmem(15, 40, 128),
                 *one, *two, *three,
                 vmem(8 * ROWS, 128), vmem(8 * ROWS, 128),
-                vmem(ny, 1, 128), vmem(13, 1, 128), vmem(3, 1, 128), vmem(2 * ny, 1, 128), vmem(nx // 2, 1, 128),
+                vmem(ny, 1, 128), vmem(9, 1, 128), vmem(3, 1, 128), vmem(2, 1, 128), vmem(2 * ny, 1, 128), vmem(nx // 2, 1, 128),
                 vmem(2 * ROWS, 128), vmem(140, 8, 128),
                 pltpu.SemaphoreType.DMA((3,)), pltpu.SemaphoreType.DMA((15,)), pltpu.SemaphoreType.DMA((15,)),
             ],

time: 50.8 us -> 54 us (1.063)
  Pallas kernels: 50 us -> 53.2 us
    pallas_call x1, Pallas kernels: 50 us -> 53.2 us  [on_device(): pl.pallas_call(functools.partial(kernel, (nx, ny)), out_shape=jax.ShapeDt...]
where the time goes in v7:
time: 54 us; the launch traced here: 53.8 us
  Pallas kernels  53.2 us (99%)
  local copies, waits for them, and re-layouts  0.63 us (1%)
    pallas_call x1, Pallas kernels, on_device(): pl.pallas_call(functools.partial(kernel, (nx, ny)), out_shape=jax.ShapeDt...  53.2 us

profile of v7, /device:TPU:1, one launch (start us, length us, event | category | flops | bytes accessed | tf_op | source)
XLA Modules:
  0.0 53.8 jit_solution(2729465933076967815)
XLA Ops:
  0.0 53.2 %shard_map.37 = f32[4,32,128]{2,1,0:T(8,128)S(1)} custom-call(f32[4,32,128]{2,1,0:T(8,128)} %source.1, f32[4,32,128]{2,1,0:T(8,128)} %beta.1, f32[4,32,128]{2,1,0:T(8,128)} %shift.1), custom_call_target="tpu_custom_call" | custom-call | tf_op jit(solution)/shard_map/pallas_call | solution.py:567
  53.2 0.6 %copy.5 = f32[4,32,128]{2,1,0:T(8,128)} copy(f32[4,32,128]{2,1,0:T(8,128)S(1)} %shard_map.37) | data formatting | bytes 131072

commit v8 on v6

--- a/solution.py
+++ b/solution.py
@@ -146,7 +146,7 @@
         else:
             start, planes = 0, min(count, reach + (dx + 1) * count)
             target = first - dx * count
-        edge = 4 if count == 1 and abs(dx) > 3 else 8
+        edge = 8 if count > 1 or abs(dx) < 4 else 4 if abs(dx) < 6 else 2
         row, high, to = (EDGE, rows, EDGE) if dy == 0 else (EDGE + rows - edge, edge, EDGE - edge) if dy > 0 else (EDGE, edge, EDGE + rows)
         out.append((dx, dy, first + start, target, planes, row, to, high))
     return out
@@ -184,13 +184,14 @@
         pltpu.make_async_copy(ref, fields.at[n, pl.ds(3, 4), pl.ds(EDGE, 32)], load_sem.at[n])
         for n, ref in enumerate((source, shift, beta))
     ]
-    for load in loads:
-        load.start()
 
     partners = sorted({(dx % nx, dy % ny) for dx, dy in wide + over_y + along_x}, key=lambda o: min(o[0], nx - o[0]) + min(o[1], ny - o[1]))
     barrier = pltpu.get_barrier_semaphore()
     for dx, dy in partners:
         pl.semaphore_signal(barrier, 1, device_id=device(-dx, -dy), device_id_type=MESH)
+
+    for load in loads:
+        load.start()
 
     def send(phase, ref, geometry, stacked):
         for dx, dy, plane, target, planes, row, to, high in geometry:

time: 50.8 us -> 50.4 us (level)
  no operation moved by 1% of the time
where the time goes in v8:
time: 50.4 us; the launch traced here: 50.2 us
  Pallas kernels  49.6 us (98%)
  local copies, waits for them, and re-layouts  0.63 us (1%)
    pallas_call x1, Pallas kernels, on_device(): pl.pallas_call(functools.partial(kernel, (nx, ny)), out_shape=jax.ShapeDt...  49.6 us

profile of v8, /device:TPU:1, one launch (start us, length us, event | category | flops | bytes accessed | tf_op | source)
XLA Modules:
  0.0 50.2 jit_solution(5603198081815929014)
XLA Ops:
  0.0 49.6 %shard_map.37 = f32[4,32,128]{2,1,0:T(8,128)S(1)} custom-call(f32[4,32,128]{2,1,0:T(8,128)} %source.1, f32[4,32,128]{2,1,0:T(8,128)} %beta.1, f32[4,32,128]{2,1,0:T(8,128)} %shift.1), custom_call_target="tpu_custom_call" | custom-call | tf_op jit(solution)/shard_map/pallas_call | solution.py:564
  49.6 0.6 %copy.5 = f32[4,32,128]{2,1,0:T(8,128)} copy(f32[4,32,128]{2,1,0:T(8,128)S(1)} %shard_map.37) | data formatting | bytes 131072
